TPU v7x, 512 devices: a whole 4x8x8 slice. The times are simulated.
512 devices in a mesh: row: 32 (over y, x), col: 16 (over z, core).
Axes of the slice: x: 4, y: 8, z: 8, core: 2. Of those that a mesh axis runs over, the one named last changes fastest.
Arguments:
- snapshots: float32 [32768, 8192], P('row', 'col'), may hold values from -400 to 400
Outputs:
- factored: float32 [32768, 8192], P('row', 'col')
- upper: float32 [512, 8192], P(None, 'col')
All inputs are finite; a program needn't handle non-finite values.
Results may differ from a plain program's by a relative error of at most 0.00018.
Values sent between devices are 32-bit elements; how exact they have to be, the bound alone decides.
No kernel may reach another device: no remote copies, remote signals or barrier semaphores. Data moves between devices by JAX's collectives and lax.ppermute only.
A program may use at most 64 MiB of HBM per device.

v0:
```python
import jax
import jax.numpy as jnp
from jax import lax
from jax.sharding import PartitionSpec as P

NB = 256


HIGH = lax.Precision.HIGHEST


def spread(value, axis, source):
    kept = jnp.where(lax.axis_index(axis) == source, value, 0).astype(value.dtype)
    return lax.psum(kept, axis)


def product_tn(left, right):
    return lax.dot_general(
        left, right, (((0,), (0,)), ((), ())), precision=HIGH, preferred_element_type=jnp.float32
    )


def product_nn(left, right):
    return jnp.dot(left, right, precision=HIGH, preferred_element_type=jnp.float32)


def body(snapshots):
    width = NB
    total_rows = snapshots.shape[0] * lax.axis_size("row")
    column = lax.axis_index("col")
    current = snapshots
    head = current[:, :width]
    bases = []
    couplings = []
    for owner in (0, 1):
        gram = lax.psum(product_tn(head, head), "row")
        gram = jnp.where(column == owner, gram / total_rows, jnp.eye(width, dtype=jnp.float32))
        lower = jnp.linalg.cholesky(gram)
        local_basis = lax.linalg.triangular_solve(
            lower, head, left_side=False, lower=True, transpose_a=True
        )
        basis = spread(local_basis, "col", owner)
        coupling = lax.psum(product_tn(basis, current), "row") / total_rows
        current = current - product_nn(basis, coupling)
        head = current[:, :width]
        bases.append(basis)
        couplings.append(coupling)
    extra = current.shape[1] - width
    inside = (jnp.arange(current.shape[1]) < width)[None, :]
    first = jnp.pad(bases[0], ((0, 0), (0, extra)))
    second = jnp.pad(bases[1], ((0, 0), (0, extra)))
    factored = jnp.where(
        inside & (column == 0), first, jnp.where(inside & (column == 1), second, current)
    )
    upper = jnp.concatenate(couplings, axis=0)
    return (factored, upper)


def solution(mesh):
    return jax.shard_map(
        body,
        mesh=mesh,
        in_specs=(P("row", "col"),),
        out_specs=(P("row", "col"), P(None, "col")),
        check_vma=False,
    )
```

profile of v0, /device:TPU:1, one launch (start us, length us, event | category | flops | bytes accessed | tf_op | source)
XLA Modules:
  0.0 1034.5 jit_solution(7672534680386777182)
XLA Ops:
  7.2 4.1 fusion.2
  11.4 156.8 %all-reduce.10.cloned.1.call-done = f32[256,256]{0,1:T(8,128)} async-done(((f32[256,256]{0,1:T(8,128)}), f32[256,256]{0,1:T(8,128)}) %all-reduce.10.cloned.1.call-update) | async-done | bytes 262160 | tf_op jit(solution)/shard_map/psum | solution.py:36
  168.2 1.0 convert_select_fusion.1
  169.3 1.1 fusion.9
  170.5 11.7 %cholesky.130 = f32[128,128]{1,0:T(8,128)S(1)} custom-call(f32[128,128]{1,0:T(8,128)S(1)} %cholesky.194), custom_call_target="Cholesky" | custom-call | tf_op jit(solution)/shard_map/jit(cholesky)/cholesky | solution.py:38
  182.2 9.8 custom-call.13
  192.5 11.7 %cholesky.147 = f32[128,128]{1,0:T(8,128)S(1)} custom-call(f32[128,128]{1,0:T(8,128)S(1)} %convolution_subtract_fusion.4), custom_call_target="Cholesky" | custom-call | tf_op jit(solution)/shard_map/jit(cholesky)/cholesky | solution.py:38
  204.3 0.7 compare_reduce_fusion.2
  206.5 4.3 while.4
  207.3 1.4 bitcast_dynamic-update-slice_fusion.4
  209.3 1.4 bitcast_dynamic-update-slice_fusion.4
  210.8 19.7 %custom-call.14 = f32[2,128,128]{1,2,0:T(8,128)S(1)} custom-call(f32[2,128,128]{2,1,0:T(8,128)S(1)} %get-tuple-element.18), custom_call_target="InvertDiagBlocksLowerTriangular" | custom-call | tf_op jit(solution)/shard_map/triangular_solve/custom-call.0 | solution.py:39
  230.4 0.6 fusion.6
  231.1 1.0 convolution_subtract_fusion.2
  232.7 1.0 maximum_select_fusion
  233.8 119.5 %all-reduce.12.cloned.1.call-done = f32[1024,256]{0,1:T(8,128)} async-done(((f32[1024,256]{0,1:T(8,128)}), f32[1024,256]{0,1:T(8,128)}) %all-reduce.12.cloned.1.call-update) | async-done | bytes 1048592 | tf_op jit(solution)/shard_map/psum | solution.py:14
  353.4 3.9 fusion.24
  357.4 1.8 copy.5
  359.2 152.1 %all-reduce.14.cloned.1.call-done = f32[256,512]{1,0:T(8,128)} async-done(((f32[256,512]{1,0:T(8,128)}), f32[256,512]{1,0:T(8,128)}) %all-reduce.14.cloned.1.call-update) | async-done | bytes 524304 | tf_op jit(solution)/shard_map/psum | solution.py:43
  511.3 3.7 convolution_subtract_fusion
  515.0 1.7 fusion
  517.0 152.3 %all-reduce.16.cloned.1.call-done = f32[256,256]{0,1:T(8,128)} async-done(((f32[256,256]{0,1:T(8,128)}), f32[256,256]{0,1:T(8,128)}) %all-reduce.16.cloned.1.call-update) | async-done | bytes 262160 | tf_op jit(solution)/shard_map/psum | solution.py:36
  669.4 1.0 convert_select_fusion
  670.4 0.8 copy.8
  671.2 1.1 fusion.8
  672.3 0.7 copy-done.5
  673.0 11.7 %cholesky.164 = f32[128,128]{1,0:T(8,128)S(1)} custom-call(f32[128,128]{1,0:T(8,128)S(1)} %cholesky.197), custom_call_target="Cholesky" | custom-call | tf_op jit(solution)/shard_map/jit(cholesky)/cholesky | solution.py:38
  684.8 9.8 custom-call.15
  694.6 1.0 constant_dynamic-update-slice_fusion.1
  695.7 1.1 convolution_subtract_fusion.3
  696.8 11.7 %cholesky.181 = f32[128,128]{1,0:T(8,128)S(1)} custom-call(f32[128,128]{1,0:T(8,128)S(1)} %convolution_subtract_fusion.3), custom_call_target="Cholesky" | custom-call | tf_op jit(solution)/shard_map/jit(cholesky)/cholesky | solution.py:38
  708.5 0.6 compare_reduce_fusion.1
  709.2 0.7 compare_reduce_fusion
  711.2 1.0 select_select_fusion.1
  712.2 4.3 while.5
  713.1 1.4 bitcast_dynamic-update-slice_fusion.5
  715.1 1.4 bitcast_dynamic-update-slice_fusion.5
  716.5 0.6 copy-done.6
  717.1 20.5 %custom-call.16 = f32[2,128,128]{1,2,0:T(8,128)S(1)} custom-call(f32[2,128,128]{2,1,0:T(8,128)} %copy-done.6), custom_call_target="InvertDiagBlocksLowerTriangular" | custom-call | tf_op jit(solution)/shard_map/triangular_solve/custom-call.0 | solution.py:39
  737.6 0.6 fusion.4
  739.5 1.0 maximum_select_fusion.1
  740.6 119.5 %all-reduce.18.cloned.1.call-done = f32[1024,256]{0,1:T(8,128)} async-done(((f32[1024,256]{0,1:T(8,128)}), f32[1024,256]{0,1:T(8,128)}) %all-reduce.18.cloned.1.call-update) | async-done | bytes 1048592 | tf_op jit(solution)/shard_map/psum | solution.py:14
  860.2 4.0 fusion.25
  864.2 1.9 broadcast_multiply_fusion.1
  866.1 151.9 %all-reduce.20.cloned.1.call-done = f32[256,512]{1,0:T(8,128)} async-done(((f32[256,512]{1,0:T(8,128)}), f32[256,512]{1,0:T(8,128)}) %all-reduce.20.cloned.1.call-update) | async-done | bytes 524304 | tf_op jit(solution)/shard_map/psum | solution.py:43
  1017.9 5.2 select_select_fusion
  1023.2 3.0 copy.10
  1026.2 1.0 pad_maximum_fusion
  (53 shorter events, 5.8 us)
Async XLA Ops:
  7.2 161.0 %all-reduce.10.cloned.1.call-start = ((), (), s32[]{:S(2)}) async-start(), calls=%async_computation | async-start | bytes 524288 | tf_op jit(solution)/shard_map/psum | solution.py:36
  11.3 342.1 %all-reduce.12.cloned.1.call-start = ((), (), s32[]{:S(2)}) async-start(), calls=%async_computation.1 | async-start | bytes 2097152 | tf_op jit(solution)/shard_map/psum | solution.py:14
  169.2 61.3 %copy-start = (f32[1024,512]{1,0:T(8,128)S(1)}, f32[1024,512]{1,0:T(8,128)}, u32[]{:S(2)}) copy-start(f32[1024,512]{1,0:T(8,128)} %param.4) | copy-start | bytes 6291460
  233.8 277.5 %all-reduce.14.cloned.1.call-start = ((), (), s32[]{:S(2)}) async-start(), calls=%async_computation.2 | async-start | bytes 1048576 | tf_op jit(solution)/shard_map/psum | solution.py:43
  357.4 154.0 %copy-start.1 = (f32[1024,256]{0,1:T(8,128)S(1)}, f32[1024,256]{0,1:T(8,128)}, u32[]{:S(2)}) copy-start(f32[1024,256]{0,1:T(8,128)} %all-reduce.12.cloned.1.call-done) | copy-start | bytes 3145732
  357.4 312.0 %all-reduce.16.cloned.1.call-start = ((), (), s32[]{:S(2)}) async-start(), calls=%async_computation.3 | async-start | bytes 524288 | tf_op jit(solution)/shard_map/psum | solution.py:36
  516.8 343.4 %all-reduce.18.cloned.1.call-start = ((), (), s32[]{:S(2)}) async-start(), calls=%async_computation.4 | async-start | bytes 2097152 | tf_op jit(solution)/shard_map/psum | solution.py:14
  672.3 0.7 copy-start.5
  709.2 2.1 copy-start.4
  716.5 0.7 copy-start.6
  740.6 277.4 %all-reduce.20.cloned.1.call-start = ((), (), s32[]{:S(2)}) async-start(), calls=%async_computation.5 | async-start | bytes 1048576 | tf_op jit(solution)/shard_map/psum | solution.py:43
  1023.2 3.0 copy-start.2
  1023.2 3.0 copy-start.3
Sparse Core Ops, SparseCore 0:
  12.0 156.1 all-reduce.9
  233.9 119.4 all-reduce.11
  357.7 153.5 all-reduce.13
  516.9 152.4 all-reduce.15
  740.7 119.4 all-reduce.17
  864.4 153.5 all-reduce.19
where the time goes:
time: 1050 us; the launch traced here: 1030 us
  waiting for transfers between devices  852 us (81%)
  other arithmetic  119 us (11%)
  matrix products  29.4 us (3%)
  between operations  17.5 us (2%)
  local copies, waits for them, and re-layouts  15.3 us (1%)
    psum x2, waiting for transfers between devices, body(): gram = lax.psum(product_tn(head, head), 'row')  309 us
    psum x2, waiting for transfers between devices, body(): coupling = lax.psum(product_tn(basis, current), 'row') / total_rows  304 us
    psum x2, waiting for transfers between devices, spread(): return lax.psum(kept, axis)  239 us
    another operation x13, other arithmetic, body(): lower = jnp.linalg.cholesky(gram)  68.7 us
    another operation x5, other arithmetic, body(): lax.linalg.triangular_solve(lower, head, left_side=False, lower=True, tra...  41.2 us
  transfers between devices with their start and end apart: 6, of which 6 were waited for; matrix products, arithmetic and copies ran while one was open for 0% of the time, Pallas kernels for 0%

commit v1 on v0

v1 whole, which is shorter than its diff:
```python
import jax
import jax.numpy as jnp
from jax import lax
from jax.experimental import pallas as pl
from jax.experimental.pallas import tpu as pltpu
from jax.sharding import PartitionSpec as P

NB = 256
BLK = 128


def lane(x, c):
    return jnp.broadcast_to(x[:, c:c + 1], (8, BLK))

def sub(x, j):
    return jnp.broadcast_to(x[j:j + 1, :], (8, BLK))

def eliminate(s, w):
    n = len(s)
    for g in range(n):
        c0 = 8 * g
        v = [lane(s[g], c0 + j) for j in range(8)]
        p = {(i, j): sub(v[j], i) for j in range(8) for i in range(j + 1)}
        r = [None] * 8
        u = {}
        hs, hw = [None] * 8, [None] * 8
        for j in range(8):
            d = p[j, j]
            r[j] = lax.rsqrt(d)
            for k in range(j + 1, 8):
                u[j, k] = p[j, k] * r[j]
            for a in range(j + 1, 8):
                for b in range(a, 8):
                    p[a, b] = p[a, b] - u[j, a] * u[j, b]
        for j in range(8):
            a, b = sub(s[g], j), sub(w[g], j)
            for m in range(j):
                a = a - u[m, j] * hs[m]
                b = b - u[m, j] * hw[m]
            hs[j], hw[j] = a * r[j], b * r[j]
        for i in range(g + 1, n):
            f = []
            for j in range(8):
                t = lane(s[i], c0 + j)
                for m in range(j):
                    t = t - f[m] * u[m, j]
                f.append(t * r[j])
            for j in range(8):
                s[i] = s[i] - f[j] * hs[j]
                w[i] = w[i] - f[j] * hw[j]
        row = lax.broadcasted_iota(jnp.int32, (8, BLK), 0)
        a, b = hs[0], hw[0]
        for j in range(1, 8):
            a = jnp.where(row == j, hs[j], a)
            b = jnp.where(row == j, hw[j], b)
        s[g], w[g] = a, b
    return s, w

def dot(a, b, dims):
    return lax.dot_general(a, b, (dims, ((), ())), precision=lax.Precision.HIGHEST, preferred_element_type=jnp.float32)

def invert(s_ref, x_ref):
    n = s_ref.shape[0]
    nb = n // BLK
    row = lax.broadcasted_iota(jnp.int32, (n, n), 0)
    col = lax.broadcasted_iota(jnp.int32, (n, n), 1)
    x_ref[...] = jnp.where(row == col, 1.0, 0.0).astype(jnp.float32)
    for k in range(nb):
        lo, hi = k * BLK, (k + 1) * BLK
        r8 = lax.broadcasted_iota(jnp.int32, (8, BLK), 0)
        c8 = lax.broadcasted_iota(jnp.int32, (8, BLK), 1)
        s = [s_ref[lo + 8 * i:lo + 8 * i + 8, lo:hi] for i in range(16)]
        w = [jnp.where(c8 == r8 + 8 * i, 1.0, 0.0).astype(jnp.float32) for i in range(16)]
        s, w = eliminate(s, w)
        inv = jnp.concatenate(w, axis=0)
        x_ref[lo:hi, lo:hi] = inv
        if k:
            x_ref[lo:hi, :lo] = dot(inv, x_ref[lo:hi, :lo], ((1,), (0,)))
        if k + 1 < nb:
            right = dot(inv, s_ref[lo:hi, hi:], ((1,), (0,)))
            s_ref[hi:, hi:] = s_ref[hi:, hi:] - dot(right, right, ((0,), (0,)))
            x_ref[hi:, :hi] = x_ref[hi:, :hi] - dot(right, x_ref[lo:hi, :hi], ((0,), (0,)))


def split(value):
    high = value.astype(jnp.bfloat16)
    return high, (value - high.astype(jnp.float32)).astype(jnp.bfloat16)


def dot3(left, right, dims):
    (a, b), (c, d) = left, right
    out = None
    for x, y in ((b, c), (a, d), (a, c)):
        term = lax.dot_general(x, y, (dims, ((), ())), preferred_element_type=jnp.float32)
        out = term if out is None else out + term
    return out


NN, NT, TN = ((1,), (0,)), ((1,), (1,)), ((0,), (0,))


def unfold(part):
    wide, rest = part[:32], part[32:]
    left = jnp.concatenate([wide[:, :NB], wide[:, NB:]], axis=0)
    right = jnp.concatenate([rest[:, BLK * i:BLK * i + BLK] for i in range(4)], axis=0)
    return left, right


def factor_kernel(core_ref, gram_ref, pair_ref, panel_ref, other_ref, inverse_ref, basis_ref, s_ref):
    even = core_ref[0] == 0
    nx = gram_ref.shape[0]
    for x in range(nx):
        rows = slice(x * 64, x * 64 + 64)
        left, right = unfold(gram_ref[x])
        left2, right2 = unfold(pair_ref[x])
        s_ref[rows, :NB] = jnp.where(even, left, left2)
        s_ref[rows, NB:NB + BLK] = jnp.where(even, right, right2)
        s_ref[rows, NB + BLK:] = jnp.where(even, right2, right)
        s_ref[NB + x * 64:NB + x * 64 + 64, NB:] = jnp.where(even, left2, left)
    invert(s_ref, inverse_ref)
    x11 = split(inverse_ref[:NB, :NB])
    x21 = split(inverse_ref[NB:, :NB])
    x22 = split(inverse_ref[NB:, NB:])

    def tile(i, carry):
        rows = pl.ds(pl.multiple_of(i * 256, 256), 256)
        mine, other = panel_ref[rows, :], other_ref[rows, :]
        one, two = split(jnp.where(even, mine, other)), split(jnp.where(even, other, mine))
        basis_ref[rows, :NB] = dot3(one, x11, NT)
        basis_ref[rows, NB:] = dot3(one, x21, NT) + dot3(two, x22, NT)
        return carry

    lax.fori_loop(0, panel_ref.shape[0] // 256, tile, 0)


def finish_kernel(column_ref, snap_ref, basis_ref, inverse_ref, inner_ref, out_ref, upper_ref, c_ref):
    column = column_ref[0]
    ny, nx, cut, _ = inner_ref.shape
    shift = (column % 2) * NB
    for x in range(nx):
        for y in range(ny):
            at = lax.rem(x * ny * cut + y * cut + shift, 2 * NB)
            c_ref[pl.ds(pl.multiple_of(at, cut), cut), :] = inner_ref[y, x]
    c1, c2 = split(c_ref[:NB, :]), split(c_ref[NB:, :])
    k1 = dot3(split(inverse_ref[:NB, :NB]), c1, NN)
    k2 = dot3(split(inverse_ref[NB:, :NB]), c1, NN) + dot3(split(inverse_ref[NB:, NB:]), c2, NN)
    upper_ref[:NB, :] = k1
    upper_ref[NB:, :] = k2
    k1, k2 = split(k1), split(k2)

    def tile(i, carry):
        rows = pl.ds(pl.multiple_of(i * 256, 256), 256)
        one, two = basis_ref[rows, :NB], basis_ref[rows, NB:]
        out = snap_ref[rows, :] - (dot3(split(one), k1, NN) + dot3(split(two), k2, NN))
        out_ref[rows, NB:] = out[:, NB:]
        own = jnp.where(column == 0, one, two)
        out_ref[rows, :NB] = jnp.where(column < 2, own, out[:, :NB])
        return carry

    lax.fori_loop(0, snap_ref.shape[0] // 256, tile, 0)


SMEM, VMEM = pl.BlockSpec(memory_space=pltpu.SMEM), pl.BlockSpec(memory_space=pltpu.VMEM)


def call(kernel, shapes, scratch, flops, *operands):
    return pl.pallas_call(
        kernel,
        out_shape=[jax.ShapeDtypeStruct(s, jnp.float32) for s in shapes],
        in_specs=[SMEM] + [VMEM] * (len(operands) - 1),
        out_specs=[VMEM] * len(shapes),
        scratch_shapes=[pltpu.VMEM(scratch, jnp.float32)],
        compiler_params=pltpu.CompilerParams(vmem_limit_bytes=48 << 20),
        cost_estimate=pl.CostEstimate(flops=flops, bytes_accessed=8 << 20, transcendentals=0),
    )(*operands)


def product(left, right, dims, precision):
    return lax.dot_general(
        left, right, (dims, ((), ())), precision=precision, preferred_element_type=jnp.float32
    )


HIGHEST, HIGH = lax.Precision.HIGHEST, lax.Precision.HIGH
NX = 4


def trade(parts, axis, groups):
    return lax.all_to_all(parts, axis, 0, 0, axis_index_groups=groups)


def copies(part, n):
    return jnp.broadcast_to(part[None], (n, *part.shape))


def fold(part):
    wide = jnp.concatenate([part[:, :32, :NB], part[:, 32:, :NB]], axis=2)
    rest = jnp.concatenate([part[:, 16 * i:16 * i + 16, NB:] for i in range(4)], axis=2)
    return jnp.concatenate([wide, rest], axis=1)


def body(snapshots):
    n_row, n_col = lax.axis_size("row"), lax.axis_size("col")
    nx, ny, nz = NX, n_row // NX, n_col // 2
    x_groups = [[y * nx + x for x in range(nx)] for y in range(ny)]
    y_groups = [[y * nx + x for y in range(ny)] for x in range(nx)]
    z_groups = [[2 * z + c for z in range(nz)] for c in range(2)]
    swap = [(i, i ^ 1) for i in range(n_col)]

    rows, width = snapshots.shape
    scale = 1.0 / (rows * n_row)
    column = lax.axis_index("col")
    core, z = column % 2, column // 2
    even = core == 0

    mine = snapshots[:, :NB]
    step = rows // nz
    piece = jnp.where(z == 0, mine[:step], 0.0)
    for k in range(1, nz):
        piece = piece + lax.ppermute(
            mine[k * step:(k + 1) * step], "col", [(c, 2 * k + c) for c in range(2)]
        )
    panel = trade(copies(piece, nz), "col", z_groups).reshape(rows, NB)

    other = lax.ppermute(panel, "col", swap)

    inner = jnp.concatenate(
        [product(panel, snapshots, TN, HIGH), product(other, snapshots, TN, HIGH)], axis=0
    )
    first = jnp.where(even, panel, other)
    second = jnp.where(even, other[:, :BLK], panel[:, BLK:])
    gram = jnp.concatenate(
        [product(panel, panel, TN, HIGHEST), product(first, second, TN, HIGHEST)], axis=1
    )
    cut = 2 * NB // nx
    gram = fold(gram.reshape(nx, NB // nx, 3 * BLK))
    inner = jnp.concatenate([inner.reshape(nx, cut, width), gram], axis=1)
    sums = jnp.sum(trade(inner, "row", x_groups), axis=0) * scale
    inner = sums[:cut].reshape(ny, cut // ny, width)
    gram = copies(sums[cut:], ny)
    sums = jnp.sum(trade(jnp.concatenate([inner, gram], axis=1), "row", y_groups), axis=0)
    cut //= ny
    parts = trade(copies(sums, nx), "row", x_groups)
    inner = trade(copies(parts[:, :cut].reshape(nx * cut, width), ny), "row", y_groups)
    gram = parts[:, cut:]

    inverse, basis = call(
        factor_kernel,
        [(2 * NB, 2 * NB), (rows, 2 * NB)],
        (2 * NB, 2 * NB),
        20 << 30,
        core.astype(jnp.int32).reshape(1), gram, lax.ppermute(gram, "col", swap), panel, other,
    )
    factored, upper = call(
        finish_kernel,
        [(rows, width), (2 * NB, width)],
        (2 * NB, width),
        4 << 30,
        column.astype(jnp.int32).reshape(1), snapshots, basis, inverse,
        inner.reshape(ny, nx, cut, width),
    )
    return (factored, upper)


def solution(mesh):
    return jax.shard_map(
        body,
        mesh=mesh,
        in_specs=(P("row", "col"),),
        out_specs=(P("row", "col"), P(None, "col")),
        check_vma=False,
    )
```

time: 1050 us -> 194 us (0.18); the launches traced: 1030 us -> 194 us
  waiting for transfers between devices: 852 us -> 7.59 us
  other arithmetic: 119 us -> 4.9 us
  blocking collectives: 0 us -> 96.9 us
  starting transfers between devices: 0.46 us -> 34.4 us
  Pallas kernels: 0 us -> 30.7 us
  matrix products: 29.4 us -> 9.24 us
  between operations: 17.5 us -> 0.99 us
    psum x6 -> x0, waiting for transfers between devices: 852 us -> none  [the longest x2 309 us: body(): gram = lax.psum(product_tn(head, head), 'row')]
    another operation x18 -> x0, other arithmetic: 110 us -> none  [the longest x13 68.7 us: body(): lower = jnp.linalg.cholesky(gram)]
    all_to_all x0 -> x4, blocking collectives: none -> 96.9 us  [trade(): return lax.all_to_all(parts, axis, 0, 0, axis_index_groups=groups)]
    pallas_call x0 -> x2, Pallas kernels: none -> 30.7 us  [call(): pl.pallas_call(kernel, out_shape=[jax.ShapeDtypeStruct(s, jnp.float32) fo...]
    ppermute x0 -> x9, starting transfers between devices: none -> 29.9 us  [the longest x7 18.7 us: body(): lax.ppermute(mine[k * step:(k + 1) * step], 'col', [(c, 2 * k + c) for c...]
    dot_general x6 -> x4, matrix products: 22.6 us -> 9.24 us  [product(): lax.dot_general(left, right, (dims, ((), ())), precision=precision, prefe...]
  transfers between devices with their start and end apart: 6 -> 10, of which waited for: 6 -> 4; matrix products, arithmetic and copies ran while one was open for 0% -> 3% of each run, Pallas kernels for 0% -> 13%
where the time goes in v1:
time: 194 us
  blocking collectives  96.9 us (50%)
  starting transfers between devices  34.4 us (18%)
  Pallas kernels  30.7 us (16%)
  matrix products  9.24 us (5%)
  local copies, waits for them, and re-layouts  8.8 us (5%)
  waiting for transfers between devices  7.59 us (4%)
  other arithmetic  4.9 us (3%)
    all_to_all x4, blocking collectives, trade(): return lax.all_to_all(parts, axis, 0, 0, axis_index_groups=groups)  96.9 us
    pallas_call x2, Pallas kernels, call(): pl.pallas_call(kernel, out_shape=[jax.ShapeDtypeStruct(s, jnp.float32) fo...  30.7 us
    ppermute x7, starting transfers between devices, body(): lax.ppermute(mine[k * step:(k + 1) * step], 'col', [(c, 2 * k + c) for c...  18.7 us
    dot_general x4, matrix products, product(): lax.dot_general(left, right, (dims, ((), ())), precision=precision, prefe...  9.24 us
    ppermute x1, starting transfers between devices, body(): other = lax.ppermute(panel, 'col', swap)  5.73 us
    ppermute x1, starting transfers between devices, body(): lax.ppermute(gram, 'col', swap)  5.53 us
    ppermute x7, waiting for transfers between devices, body(): lax.ppermute(mine[k * step:(k + 1) * step], 'col', [(c, 2 * k + c) for c...  5.11 us
    unnamed x12, local copies, waits for them, and re-layouts  4.5 us
  transfers between devices with their start and end apart: 10, of which 4 were waited for; matrix products, arithmetic and copies ran while one was open for 3% of the time, Pallas kernels for 13%

profile of v1, /device:TPU:1, one launch (start us, length us, event | category | flops | bytes accessed | tf_op | source)
XLA Modules:
  0.0 193.5 jit_solution(5525698596774508568)
XLA Ops:
  0.6 1.3 fusion.5
  2.0 4.8 %collective-permute-start = (f32[128,256]{1,0:T(8,128)S(1)}, f32[128,256]{1,0:T(8,128)S(1)}, u32[]{:S(2)}, u32[]{:S(2)}) collective-permute-start(f32[128,256]{1,0:T(8,128)S(1)} %get-tuple-element.6), channel_id=1, source_target_pairs={{0,2},{1,3},{16,18},{17,19},{32,34},{33,35},{48,50},{49,51},{64,66... | collective-permute-start | bytes 393224 | tf_op jit(solution)/shard_map/ppermute | solution.py:220
  6.8 7.3 %collective-permute-start.6 = (f32[128,256]{1,0:T(8,128)S(1)}, f32[128,256]{1,0:T(8,128)S(1)}, u32[]{:S(2)}, u32[]{:S(2)}) collective-permute-start(f32[128,256]{1,0:T(8,128)S(1)} %get-tuple-element.7), channel_id=1, source_target_pairs={{0,14},{1,15},{16,30},{17,31},{32,46},{33,47},{48,62},{49,63},{64,... | collective-permute-start | bytes 393224 | tf_op jit(solution)/shard_map/ppermute | solution.py:220
  14.1 1.3 collective-permute-start.5
  15.5 1.3 collective-permute-start.4
  16.8 1.3 collective-permute-start.3
  18.1 1.3 collective-permute-start.2
  19.4 0.0 collective-permute-done.6
  19.4 1.3 collective-permute-start.1
  20.7 0.0 collective-permute-done.5
  20.7 1.2 collective-permute-done.4
  21.9 0.0 collective-permute-done.3
  21.9 1.1 collective-permute-done.2
  23.0 2.8 %collective-permute-done.1 = f32[128,256]{1,0:T(8,128)S(1)} collective-permute-done((f32[128,256]{1,0:T(8,128)S(1)}, f32[128,256]{1,0:T(8,128)S(1)}, u32[]{:S(2)}, u32[]{:S(2)}) %collective-permute-start.1) | collective-permute-done | bytes 131104 | tf_op jit(solution)/shard_map/ppermute | solution.py:220
  25.8 1.0 add_add_fusion
  26.8 0.1 copy.16
  26.9 0.1 broadcast_in_dim.15
  27.0 30.2 %all_to_all.25 = f32[8,128,256]{1,2,0:T(8,128)S(1)} all-to-all(f32[8,128,256]{1,2,0:T(8,128)S(1)} %broadcast_in_dim.15), channel_id=1, replica_groups={{0,2,4,6,8,10,12,14},{1,3,5,7,9,11,13,15},{16,18,20,22,24,26,28,30},{17..., dimensions={0} | all-to-all | bytes 2097152 | tf_op jit(solution)/shard_map/all_to_all | solution.py:189
  57.1 1.0 copy-done.4
  58.1 0.3 copy.17
  58.4 0.0 copy-start
  58.5 5.7 %collective-permute-start.7 = (f32[1024,256]{1,0:T(8,128)S(1)}, f32[1024,256]{1,0:T(8,128)}, u32[]{:S(2)}, u32[]{:S(2)}) collective-permute-start(f32[1024,256]{1,0:T(8,128)S(1)} %bitcast.16), channel_id=1, source_target_pairs={{0,1},{1,0},{2,3},{3,2},{4,5},{5,4},{6,7},{7,6},{8,9},{9,8},{10,11... | collective-permute-start | bytes 3145736 | tf_op jit(solution)/shard_map/ppermute | solution.py:225
  64.2 2.6 %convolution_bitcast_fusion = f32[256,256]{0,1:T(8,128)S(1)} fusion(f32[8,128,256]{1,2,0:T(8,128)} %copy-done.4), kind=kOutput, calls=%fused_computation.1 | convolution fusion | flops 805306368 | bytes 1310720 | tf_op jit(solution)/shard_map/dot_general | solution.py:179
  66.8 1.8 fusion.8
  68.7 2.5 %fusion = f32[256,128]{0,1:T(8,128)S(1)} fusion(f32[1024,256]{1,0:T(8,128)S(1)} %bitcast.18, f32[1024,256]{1,0:T(8,128)} %collective-permute-done.7.other_ref, pred[]{:T(512)S(6)} %eq.9), kind=kOutput, calls=%fused_computation.4 | convolution fusion | flops 403046400 | bytes 3277824 | tf_op jit(solution)/shard_map/dot_general | solution.py:179
  71.2 0.8 pad_maximum_fusion.2
  71.9 1.2 copy.19
  73.2 0.0 copy-start.5
  73.2 2.3 %fusion.9 = f32[256,512]{1,0:T(8,128)S(1)} fusion(f32[1024,256]{1,0:T(8,128)} %collective-permute-done.7.other_ref, f32[1024,512]{1,0:T(8,128)S(1)} %copy-done), kind=kOutput, calls=%fused_computation.17 | convolution fusion | flops 805306368 | bytes 3670016 | tf_op jit(solution)/shard_map/dot_general | solution.py:179
  75.5 0.1 pad_maximum_fusion
  75.6 0.1 maximum_maximum_fusion
  75.7 23.5 %all_to_all.26 = f32[4,176,512]{2,1,0:T(8,128)} all-to-all(f32[4,176,512]{2,1,0:T(8,128)S(1)} %maximum_maximum_fusion), channel_id=1, replica_groups={{0,16,32,48},{64,80,96,112},{128,144,160,176},{192,208,224,240},{256,27..., dimensions={0} | all-to-all | bytes 2883584 | tf_op jit(solution)/shard_map/all_to_all | solution.py:189
  99.2 1.5 reduce_sum.18
  100.9 0.1 broadcast_in_dim.16
  100.9 0.1 pad_maximum_fusion.1
  101.0 33.9 %all_to_all.27 = f32[8,64,512]{2,1,0:T(8,128)} all-to-all(f32[8,64,512]{2,1,0:T(8,128)S(1)} %pad_maximum_fusion.1), channel_id=1, replica_groups={{0,64,128,192,256,320,384,448},{16,80,144,208,272,336,400,464},{32,96,1..., dimensions={0} | all-to-all | bytes 2097152 | tf_op jit(solution)/shard_map/all_to_all | solution.py:189
  134.9 1.3 reduce_sum.19
  136.2 0.1 broadcast_in_dim.32
  136.3 9.3 %all_to_all.28 = f32[4,64,512]{2,1,0:T(8,128)S(1)} all-to-all(f32[4,64,512]{2,1,0:T(8,128)S(1)} %broadcast_in_dim.32), channel_id=1, replica_groups={{0,16,32,48},{64,80,96,112},{128,144,160,176},{192,208,224,240},{256,27..., dimensions={0} | all-to-all | bytes 1048576 | tf_op jit(solution)/shard_map/all_to_all | solution.py:189
  145.7 5.5 %collective-permute-start.8 = (f32[4,48,512]{2,1,0:T(8,128)S(1)}, f32[4,48,512]{2,1,0:T(8,128)}, u32[]{:S(2)}, u32[]{:S(2)}) collective-permute-start(f32[4,48,512]{2,1,0:T(8,128)S(1)} %slice.99.gram_ref), channel_id=1, source_target_pairs={{0,1},{1,0},{2,3},{3,2},{4,5},{5,4},{6,7},{7,6},{8,9},{9,8},{10,11... | collective-permute-start | bytes 1179656 | tf_op jit(solution)/shard_map/ppermute | solution.py:252
  151.2 1.1 broadcast_in_dim.34
  152.3 4.4 %all-to-all-start.4 = ((f32[8,64,512]{2,1,0:T(8,128)}), f32[8,64,512]{2,1,0:T(8,128)}, u32[]{:S(2)}, u32[]{:S(2)}) async-start(f32[8,64,512]{2,1,0:T(8,128)} %broadcast_in_dim.34), calls=%async_computation.4 | async-start | bytes 2097152 | tf_op jit(solution)/shard_map/all_to_all | solution.py:189
  156.8 24.3 %shard_map.30 = (f32[512,512]{1,0:T(8,128)S(1)}, f32[1024,512]{1,0:T(8,128)S(1)}) custom-call(s32[1]{0:T(128)} %bitcast.1.core_ref, f32[4,48,512]{2,1,0:T(8,128)S(1)} %slice.99.gram_ref, f32[4,48,512]{2,1,0:T(8,128)} %collective-permute-done.8.pair_ref, f32[1024,256]{1,0:T(8,128)S(1)} %bitcast.19, f32[1024,256]{1,0:T(8,128)} %collective-permute-done.7.other_ref), custom_call_target="tpu_custom_call" | custom-call | flops 21474836480 | bytes 8388608 | tf_op jit(solution)/shard_map/pallas_call | solution.py:167
  181.1 1.3 copy-done.1
  182.4 1.0 copy-done.2
  183.4 2.5 %all-to-all-done.4 = f32[8,64,512]{2,1,0:T(8,128)} async-done(((f32[8,64,512]{2,1,0:T(8,128)}), f32[8,64,512]{2,1,0:T(8,128)}, u32[]{:S(2)}, u32[]{:S(2)}) %all-to-all-start.4) | async-done | bytes 1048608 | tf_op jit(solution)/shard_map/all_to_all | solution.py:189
  185.9 1.2 copy-done.3
  187.1 6.4 %shard_map.31 = (f32[1024,512]{1,0:T(8,128)}, f32[512,512]{1,0:T(8,128)}) custom-call(s32[1]{0:T(128)} %bitcast.column_ref, f32[1024,512]{1,0:T(8,128)S(1)} %copy-done, f32[1024,512]{1,0:T(8,128)} %copy-done.1, f32[512,512]{1,0:T(8,128)S(1)} %copy-done.3, f32[8,4,16,512]{3,2,1,0:T(8,128)} %bitcast.8.inner_ref), custom_call_target="tpu_custom_call" | custom-call | flops 4294967296 | bytes 8388608 | tf_op jit(solution)/shard_map/pallas_call | solution.py:167
  (16 shorter events, 0.1 us)
Async XLA Ops:
  2.0 16.1 %collective-permute-start = (f32[128,256]{1,0:T(8,128)S(1)}, f32[128,256]{1,0:T(8,128)S(1)}, u32[]{:S(2)}, u32[]{:S(2)}) collective-permute-start(f32[128,256]{1,0:T(8,128)S(1)} %get-tuple-element.6), channel_id=1, source_target_pairs={{0,2},{1,3},{16,18},{17,19},{32,34},{33,35},{48,50},{49,51},{64,66... | collective-permute-start | bytes 393224 | tf_op jit(solution)/shard_map/ppermute | solution.py:220
  6.8 12.6 %collective-permute-start.6 = (f32[128,256]{1,0:T(8,128)S(1)}, f32[128,256]{1,0:T(8,128)S(1)}, u32[]{:S(2)}, u32[]{:S(2)}) collective-permute-start(f32[128,256]{1,0:T(8,128)S(1)} %get-tuple-element.7), channel_id=1, source_target_pairs={{0,14},{1,15},{16,30},{17,31},{32,46},{33,47},{48,62},{49,63},{64,... | collective-permute-start | bytes 393224 | tf_op jit(solution)/shard_map/ppermute | solution.py:220
  14.1 6.6 %collective-permute-start.5 = (f32[128,256]{1,0:T(8,128)S(1)}, f32[128,256]{1,0:T(8,128)S(1)}, u32[]{:S(2)}, u32[]{:S(2)}) collective-permute-start(f32[128,256]{1,0:T(8,128)S(1)} %get-tuple-element.8), channel_id=1, source_target_pairs={{0,12},{1,13},{16,28},{17,29},{32,44},{33,45},{48,60},{49,61},{64,... | collective-permute-start | bytes 393224 | tf_op jit(solution)/shard_map/ppermute | solution.py:220
  15.5 6.5 %collective-permute-start.4 = (f32[128,256]{1,0:T(8,128)S(1)}, f32[128,256]{1,0:T(8,128)S(1)}, u32[]{:S(2)}, u32[]{:S(2)}) collective-permute-start(f32[128,256]{1,0:T(8,128)S(1)} %get-tuple-element.9), channel_id=1, source_target_pairs={{0,10},{1,11},{16,26},{17,27},{32,42},{33,43},{48,58},{49,59},{64,... | collective-permute-start | bytes 393224 | tf_op jit(solution)/shard_map/ppermute | solution.py:220
  16.8 5.2 %collective-permute-start.3 = (f32[128,256]{1,0:T(8,128)S(1)}, f32[128,256]{1,0:T(8,128)S(1)}, u32[]{:S(2)}, u32[]{:S(2)}) collective-permute-start(f32[128,256]{1,0:T(8,128)S(1)} %get-tuple-element.10), channel_id=1, source_target_pairs={{0,8},{1,9},{16,24},{17,25},{32,40},{33,41},{48,56},{49,57},{64,72... | collective-permute-start | bytes 393224 | tf_op jit(solution)/shard_map/ppermute | solution.py:220
  18.1 4.9 %collective-permute-start.2 = (f32[128,256]{1,0:T(8,128)S(1)}, f32[128,256]{1,0:T(8,128)S(1)}, u32[]{:S(2)}, u32[]{:S(2)}) collective-permute-start(f32[128,256]{1,0:T(8,128)S(1)} %get-tuple-element.11), channel_id=1, source_target_pairs={{0,6},{1,7},{16,22},{17,23},{32,38},{33,39},{48,54},{49,55},{64,70... | collective-permute-start | bytes 393224 | tf_op jit(solution)/shard_map/ppermute | solution.py:220
  19.4 6.4 %collective-permute-start.1 = (f32[128,256]{1,0:T(8,128)S(1)}, f32[128,256]{1,0:T(8,128)S(1)}, u32[]{:S(2)}, u32[]{:S(2)}) collective-permute-start(f32[128,256]{1,0:T(8,128)S(1)} %get-tuple-element.12), channel_id=1, source_target_pairs={{0,4},{1,5},{16,20},{17,21},{32,36},{33,37},{48,52},{49,53},{64,68... | collective-permute-start | bytes 393224 | tf_op jit(solution)/shard_map/ppermute | solution.py:220
  57.1 1.0 copy-start.4
  58.4 8.4 %copy-start = (f32[1024,512]{1,0:T(8,128)S(1)}, f32[1024,512]{1,0:T(8,128)}, u32[]{:S(2)}) copy-start(f32[1024,512]{1,0:T(8,128)} %snap_ref.1) | copy-start | bytes 6291460
  58.5 10.2 %collective-permute-start.7 = (f32[1024,256]{1,0:T(8,128)S(1)}, f32[1024,256]{1,0:T(8,128)}, u32[]{:S(2)}, u32[]{:S(2)}) collective-permute-start(f32[1024,256]{1,0:T(8,128)S(1)} %bitcast.16), channel_id=1, source_target_pairs={{0,1},{1,0},{2,3},{3,2},{4,5},{5,4},{6,7},{7,6},{8,9},{9,8},{10,11... | collective-permute-start | bytes 3145736 | tf_op jit(solution)/shard_map/ppermute | solution.py:225
  73.2 2.3 %copy-start.5 = (f32[256,512]{1,0:T(8,128)S(1)}, f32[256,512]{1,0:T(8,128)}, u32[]{:S(2)}) copy-start(f32[256,512]{1,0:T(8,128)} %fusion.8) | copy-start | bytes 1572868
  145.7 11.1 %collective-permute-start.8 = (f32[4,48,512]{2,1,0:T(8,128)S(1)}, f32[4,48,512]{2,1,0:T(8,128)}, u32[]{:S(2)}, u32[]{:S(2)}) collective-permute-start(f32[4,48,512]{2,1,0:T(8,128)S(1)} %slice.99.gram_ref), channel_id=1, source_target_pairs={{0,1},{1,0},{2,3},{3,2},{4,5},{5,4},{6,7},{7,6},{8,9},{9,8},{10,11... | collective-permute-start | bytes 1179656 | tf_op jit(solution)/shard_map/ppermute | solution.py:252
  152.3 33.5 %all-to-all-start.4 = ((f32[8,64,512]{2,1,0:T(8,128)}), f32[8,64,512]{2,1,0:T(8,128)}, u32[]{:S(2)}, u32[]{:S(2)}) async-start(f32[8,64,512]{2,1,0:T(8,128)} %broadcast_in_dim.34), calls=%async_computation.4 | async-start | bytes 2097152 | tf_op jit(solution)/shard_map/all_to_all | solution.py:189
  181.1 1.3 copy-start.1
  182.4 1.0 copy-start.2
  185.9 1.2 copy-start.3

commit v2 on v1

--- a/solution.py
+++ b/solution.py
@@ -99,65 +99,79 @@
 NN, NT, TN = ((1,), (0,)), ((1,), (1,)), ((0,), (0,))
 
 
-def unfold(part):
-    wide, rest = part[:32], part[32:]
-    left = jnp.concatenate([wide[:, :NB], wide[:, NB:]], axis=0)
-    right = jnp.concatenate([rest[:, BLK * i:BLK * i + BLK] for i in range(4)], axis=0)
-    return left, right
-
-
-def factor_kernel(core_ref, gram_ref, pair_ref, panel_ref, other_ref, inverse_ref, basis_ref, s_ref):
+def inner_kernel(column_ref, snap_ref, panel_ref, other_ref, out_ref, gram_ref):
+    column = column_ref[0]
+    even, z = column % 2 == 0, column // 2
+    nx, tall, width = out_ref.shape
+    cut = 2 * NB // nx
+    mine, other = panel_ref[...], other_ref[...]
+    snap = split(snap_ref[...])
+    for k, part in enumerate((mine, other)):
+        inner = dot3(split(part), snap, TN)
+        for x in range(nx // 2):
+            out_ref[k * nx // 2 + x, :cut, :] = inner[x * cut:x * cut + cut]
+    first = jnp.where(even, mine, other)
+    second = jnp.where(even, other[:, :BLK], mine[:, BLK:])
+    gram_ref[:, :NB], gram_ref[:, NB:] = dot(mine, mine, TN), dot(first, second, TN)
+    for x in range(nx):
+        rows = pl.ds(pl.multiple_of(x * (NB // nx) + z * 8, 8), 8)
+        out_ref[x, cut:cut + 8, :3 * BLK] = gram_ref[rows, :]
+        out_ref[x, cut:cut + 8, 3 * BLK:] = jnp.zeros((8, width - 3 * BLK), jnp.float32)
+        out_ref[x, cut + 8:, :] = jnp.zeros((tall - cut - 8, width), jnp.float32)
+
+
+def factor_kernel(core_ref, gram_ref, pair_ref, inverse_ref, s_ref):
     even = core_ref[0] == 0
     nx = gram_ref.shape[0]
     for x in range(nx):
         rows = slice(x * 64, x * 64 + 64)
-        left, right = unfold(gram_ref[x])
-        left2, right2 = unfold(pair_ref[x])
+        left, right = gram_ref[x, :, :NB], gram_ref[x, :, NB:3 * BLK]
+        left2, right2 = pair_ref[x, :, :NB], pair_ref[x, :, NB:3 * BLK]
         s_ref[rows, :NB] = jnp.where(even, left, left2)
         s_ref[rows, NB:NB + BLK] = jnp.where(even, right, right2)
         s_ref[rows, NB + BLK:] = jnp.where(even, right2, right)
         s_ref[NB + x * 64:NB + x * 64 + 64, NB:] = jnp.where(even, left2, left)
     invert(s_ref, inverse_ref)
-    x11 = split(inverse_ref[:NB, :NB])
-    x21 = split(inverse_ref[NB:, :NB])
-    x22 = split(inverse_ref[NB:, NB:])
-
-    def tile(i, carry):
-        rows = pl.ds(pl.multiple_of(i * 256, 256), 256)
-        mine, other = panel_ref[rows, :], other_ref[rows, :]
-        one, two = split(jnp.where(even, mine, other)), split(jnp.where(even, other, mine))
-        basis_ref[rows, :NB] = dot3(one, x11, NT)
-        basis_ref[rows, NB:] = dot3(one, x21, NT) + dot3(two, x22, NT)
-        return carry
-
-    lax.fori_loop(0, panel_ref.shape[0] // 256, tile, 0)
-
-
-def finish_kernel(column_ref, snap_ref, basis_ref, inverse_ref, inner_ref, out_ref, upper_ref, c_ref):
+
+
+def finish_kernel(
+    column_ref, snap_ref, panel_ref, other_ref, inverse_ref, inner_ref, out_ref, upper_ref, c_ref, half_ref
+):
     column = column_ref[0]
+    even = column % 2 == 0
     ny, nx, cut, _ = inner_ref.shape
-    shift = (column % 2) * NB
-    for x in range(nx):
-        for y in range(ny):
-            at = lax.rem(x * ny * cut + y * cut + shift, 2 * NB)
-            c_ref[pl.ds(pl.multiple_of(at, cut), cut), :] = inner_ref[y, x]
-    c1, c2 = split(c_ref[:NB, :]), split(c_ref[NB:, :])
-    k1 = dot3(split(inverse_ref[:NB, :NB]), c1, NN)
-    k2 = dot3(split(inverse_ref[NB:, :NB]), c1, NN) + dot3(split(inverse_ref[NB:, NB:]), c2, NN)
-    upper_ref[:NB, :] = k1
-    upper_ref[NB:, :] = k2
-    k1, k2 = split(k1), split(k2)
-
-    def tile(i, carry):
-        rows = pl.ds(pl.multiple_of(i * 256, 256), 256)
-        one, two = basis_ref[rows, :NB], basis_ref[rows, NB:]
-        out = snap_ref[rows, :] - (dot3(split(one), k1, NN) + dot3(split(two), k2, NN))
-        out_ref[rows, NB:] = out[:, NB:]
-        own = jnp.where(column == 0, one, two)
-        out_ref[rows, :NB] = jnp.where(column < 2, own, out[:, :NB])
-        return carry
-
-    lax.fori_loop(0, snap_ref.shape[0] // 256, tile, 0)
+    blocks = ((slice(0, NB), slice(0, NB)), (slice(NB, 2 * NB), slice(0, NB)), (slice(NB, 2 * NB), slice(NB, 2 * NB)))
+
+    @pl.when(pl.program_id(0) == 0)
+    def _():
+        shift = (column % 2) * NB
+        for x in range(nx):
+            for y in range(ny):
+                at = lax.rem(x * ny * cut + y * cut + shift, 2 * NB)
+                c_ref[pl.ds(pl.multiple_of(at, cut), cut), :] = inner_ref[y, x]
+        x11, x21, x22 = (split(inverse_ref[b]) for b in blocks)
+        c1, c2 = split(c_ref[:NB, :]), split(c_ref[NB:, :])
+        k1 = dot3(x11, c1, NN)
+        k2 = dot3(x21, c1, NN) + dot3(x22, c2, NN)
+        upper_ref[:NB, :] = k1
+        upper_ref[NB:, :] = k2
+        for i, part in enumerate((x11, x21, x22)):
+            half_ref[2 * i], half_ref[2 * i + 1] = part[0], part[1]
+        for i, k in enumerate((k1, k2)):
+            for j, part in enumerate(split(k)):
+                half_ref[6 + 2 * i + j], half_ref[10 + 2 * i + j] = part[:, :NB], part[:, NB:]
+
+    x11, x21, x22 = ((half_ref[2 * i], half_ref[2 * i + 1]) for i in range(3))
+    mine, other = panel_ref[...], other_ref[...]
+    one, two = split(jnp.where(even, mine, other)), split(jnp.where(even, other, mine))
+    one, two = dot3(one, x11, NT), dot3(one, x21, NT) + dot3(two, x22, NT)
+    own = jnp.where(column == 0, one, two)
+    one, two = split(one), split(two)
+    for h in range(2):
+        at = slice(h * NB, h * NB + NB)
+        k1, k2 = ((half_ref[6 + 4 * h + 2 * i], half_ref[7 + 4 * h + 2 * i]) for i in range(2))
+        out = snap_ref[:, at] - (dot3(one, k1, NN) + dot3(two, k2, NN))
+        out_ref[:, at] = jnp.where(column < 2, own, out) if h == 0 else out
 
 
 SMEM, VMEM = pl.BlockSpec(memory_space=pltpu.SMEM), pl.BlockSpec(memory_space=pltpu.VMEM)
@@ -169,19 +183,39 @@
         out_shape=[jax.ShapeDtypeStruct(s, jnp.float32) for s in shapes],
         in_specs=[SMEM] + [VMEM] * (len(operands) - 1),
         out_specs=[VMEM] * len(shapes),
-        scratch_shapes=[pltpu.VMEM(scratch, jnp.float32)],
-        compiler_params=pltpu.CompilerParams(vmem_limit_bytes=48 << 20),
+        scratch_shapes=[pltpu.VMEM(s, jnp.float32) for s in scratch],
+        compiler_params=pltpu.CompilerParams(vmem_limit_bytes=24 << 20),
         cost_estimate=pl.CostEstimate(flops=flops, bytes_accessed=8 << 20, transcendentals=0),
     )(*operands)
 
 
-def product(left, right, dims, precision):
-    return lax.dot_general(
-        left, right, (dims, ((), ())), precision=precision, preferred_element_type=jnp.float32
-    )
-
-
-HIGHEST, HIGH = lax.Precision.HIGHEST, lax.Precision.HIGH
+def finish(column, snapshots, panel, other, inverse, inner):
+    rows, width = snapshots.shape
+    tile = 256
+
+    def whole(shape):
+        return pl.BlockSpec(shape, lambda i: (0,) * len(shape))
+
+    def tiles(columns):
+        return pl.BlockSpec((tile, columns), lambda i: (i, 0))
+
+    return pl.pallas_call(
+        finish_kernel,
+        grid=(rows // tile,),
+        out_shape=[
+            jax.ShapeDtypeStruct((rows, width), jnp.float32),
+            jax.ShapeDtypeStruct((2 * NB, width), jnp.float32),
+        ],
+        in_specs=[SMEM, tiles(width), tiles(NB), tiles(NB), whole(inverse.shape), whole(inner.shape)],
+        out_specs=[tiles(width), whole((2 * NB, width))],
+        scratch_shapes=[
+            pltpu.VMEM((2 * NB, width), jnp.float32), pltpu.VMEM((14, NB, NB), jnp.bfloat16)
+        ],
+        compiler_params=pltpu.CompilerParams(vmem_limit_bytes=60 << 20),
+        cost_estimate=pl.CostEstimate(flops=4 << 30, bytes_accessed=8 << 20, transcendentals=0),
+    )(column, snapshots, panel, other, inverse, inner)
+
+
 NX = 4
 
 
@@ -191,12 +225,6 @@
 
 def copies(part, n):
     return jnp.broadcast_to(part[None], (n, *part.shape))
-
-
-def fold(part):
-    wide = jnp.concatenate([part[:, :32, :NB], part[:, 32:, :NB]], axis=2)
-    rest = jnp.concatenate([part[:, 16 * i:16 * i + 16, NB:] for i in range(4)], axis=2)
-    return jnp.concatenate([wide, rest], axis=1)
 
 
 def body(snapshots):
@@ -210,8 +238,7 @@
     rows, width = snapshots.shape
     scale = 1.0 / (rows * n_row)
     column = lax.axis_index("col")
-    core, z = column % 2, column // 2
-    even = core == 0
+    z = column // 2
 
     mine = snapshots[:, :NB]
     step = rows // nz
@@ -224,39 +251,30 @@
 
     other = lax.ppermute(panel, "col", swap)
 
-    inner = jnp.concatenate(
-        [product(panel, snapshots, TN, HIGH), product(other, snapshots, TN, HIGH)], axis=0
-    )
-    first = jnp.where(even, panel, other)
-    second = jnp.where(even, other[:, :BLK], panel[:, BLK:])
-    gram = jnp.concatenate(
-        [product(panel, panel, TN, HIGHEST), product(first, second, TN, HIGHEST)], axis=1
-    )
+    place = column.astype(jnp.int32).reshape(1)
     cut = 2 * NB // nx
-    gram = fold(gram.reshape(nx, NB // nx, 3 * BLK))
-    inner = jnp.concatenate([inner.reshape(nx, cut, width), gram], axis=1)
+    inner, = call(
+        inner_kernel, [(nx, cut + 16, width)], [(NB, 3 * BLK)], 4 << 30, place, snapshots, panel, other
+    )
     sums = jnp.sum(trade(inner, "row", x_groups), axis=0) * scale
     inner = sums[:cut].reshape(ny, cut // ny, width)
-    gram = copies(sums[cut:], ny)
+    gram = copies(sums[cut:cut + 8], ny)
+    cut //= ny
     sums = jnp.sum(trade(jnp.concatenate([inner, gram], axis=1), "row", y_groups), axis=0)
-    cut //= ny
-    parts = trade(copies(sums, nx), "row", x_groups)
+    gram = trade(copies(sums[cut:], nz), "col", z_groups).reshape(8 * nz, width)
+    parts = trade(copies(jnp.concatenate([sums[:cut], gram], axis=0), nx), "row", x_groups)
     inner = trade(copies(parts[:, :cut].reshape(nx * cut, width), ny), "row", y_groups)
     gram = parts[:, cut:]
 
-    inverse, basis = call(
+    inverse, = call(
         factor_kernel,
-        [(2 * NB, 2 * NB), (rows, 2 * NB)],
-        (2 * NB, 2 * NB),
+        [(2 * NB, 2 * NB)],
+        [(2 * NB, 2 * NB)],
         20 << 30,
-        core.astype(jnp.int32).reshape(1), gram, lax.ppermute(gram, "col", swap), panel, other,
-    )
-    factored, upper = call(
-        finish_kernel,
-        [(rows, width), (2 * NB, width)],
-        (2 * NB, width),
-        4 << 30,
-        column.astype(jnp.int32).reshape(1), snapshots, basis, inverse,
+        place % 2, gram, lax.ppermute(gram, "col", swap),
+    )
+    factored, upper = finish(
+        place, snapshots, panel, other, inverse,
         inner.reshape(ny, nx, cut, width),
     )
     return (factored, upper)

time: 194 us -> 180 us (0.928)
  blocking collectives: 96.9 us -> 78 us
  waiting for transfers between devices: 7.59 us -> 21.8 us
  matrix products: 9.24 us -> 0 us
  starting transfers between devices: 34.4 us -> 40.2 us
  other arithmetic: 4.9 us -> 1.23 us
  local copies, waits for them, and re-layouts: 8.8 us -> 5.28 us
    all_to_all x4, blocking collectives: 96.9 us -> 78 us  [trade(): return lax.all_to_all(parts, axis, 0, 0, axis_index_groups=groups)]
    all_to_all x1 -> x2, waiting for transfers between devices: 2.48 us -> 15 us  [trade(): return lax.all_to_all(parts, axis, 0, 0, axis_index_groups=groups)]
    dot_general x4 -> x0, matrix products: 9.24 us -> none  [product(): lax.dot_general(left, right, (dims, ((), ())), precision=precision, prefe...]
    pallas_call x0 -> x1, Pallas kernels: none -> 7.94 us  [finish(): pl.pallas_call(finish_kernel, grid=(rows // tile,), out_shape=[jax.ShapeD...]
    pallas_call x2, Pallas kernels: 30.7 us -> 24.5 us  [call(): pl.pallas_call(kernel, out_shape=[jax.ShapeDtypeStruct(s, jnp.float32) fo...]
    ppermute x1, starting transfers between devices: 5.53 us -> 8.22 us  [body(): lax.ppermute(gram, 'col', swap)]
    all_to_all x1 -> x2, starting transfers between devices: 4.43 us -> 7.11 us  [trade(): return lax.all_to_all(parts, axis, 0, 0, axis_index_groups=groups)]
    unnamed x12 -> x10, local copies, waits for them, and re-layouts: 4.5 us -> 1.97 us
  transfers between devices with their start and end apart: 10 -> 11, of which waited for: 4 -> 6; matrix products, arithmetic and copies ran while one was open for 3% -> 1% of each run, Pallas kernels for 13% -> 12%
where the time goes in v2:
time: 180 us
  blocking collectives  78 us (43%)
  starting transfers between devices  40.2 us (22%)
  Pallas kernels  32.4 us (18%)
  waiting for transfers between devices  21.8 us (12%)
  local copies, waits for them, and re-layouts  5.28 us (3%)
    all_to_all x4, blocking collectives, trade(): return lax.all_to_all(parts, axis, 0, 0, axis_index_groups=groups)  78 us
    pallas_call x2, Pallas kernels, call(): pl.pallas_call(kernel, out_shape=[jax.ShapeDtypeStruct(s, jnp.float32) fo...  24.5 us
    ppermute x7, starting transfers between devices, body(): lax.ppermute(mine[k * step:(k + 1) * step], 'col', [(c, 2 * k + c) for c...  19.3 us
    all_to_all x2, waiting for transfers between devices, trade(): return lax.all_to_all(parts, axis, 0, 0, axis_index_groups=groups)  15 us
    ppermute x1, starting transfers between devices, body(): lax.ppermute(gram, 'col', swap)  8.22 us
    pallas_call x1, Pallas kernels, finish(): pl.pallas_call(finish_kernel, grid=(rows // tile,), out_shape=[jax.ShapeD...  7.94 us
    all_to_all x2, starting transfers between devices, trade(): return lax.all_to_all(parts, axis, 0, 0, axis_index_groups=groups)  7.11 us
    ppermute x1, starting transfers between devices, body(): other = lax.ppermute(panel, 'col', swap)  5.59 us
  transfers between devices with their start and end apart: 11, of which 6 were waited for; matrix products, arithmetic and copies ran while one was open for 1% of the time, Pallas kernels for 12%

profile of v2, /device:TPU:1, one launch (start us, length us, event | category | flops | bytes accessed | tf_op | source)
XLA Modules:
  0.0 179.8 jit_solution(10588744025679655960)
XLA Ops:
  0.6 1.3 fusion
  1.9 4.8 %collective-permute-start = (f32[128,256]{1,0:T(8,128)S(1)}, f32[128,256]{1,0:T(8,128)S(1)}, u32[]{:S(2)}, u32[]{:S(2)}) collective-permute-start(f32[128,256]{1,0:T(8,128)S(1)} %get-tuple-element.2), channel_id=1, source_target_pairs={{0,2},{1,3},{16,18},{17,19},{32,34},{33,35},{48,50},{49,51},{64,66... | collective-permute-start | bytes 393224 | tf_op jit(solution)/shard_map/ppermute | solution.py:247
  6.8 7.3 %collective-permute-start.6 = (f32[128,256]{1,0:T(8,128)S(1)}, f32[128,256]{1,0:T(8,128)S(1)}, u32[]{:S(2)}, u32[]{:S(2)}) collective-permute-start(f32[128,256]{1,0:T(8,128)S(1)} %get-tuple-element.3), channel_id=1, source_target_pairs={{0,14},{1,15},{16,30},{17,31},{32,46},{33,47},{48,62},{49,63},{64,... | collective-permute-start | bytes 393224 | tf_op jit(solution)/shard_map/ppermute | solution.py:247
  14.1 1.3 collective-permute-start.5
  15.4 1.3 collective-permute-start.4
  16.7 1.3 collective-permute-start.3
  18.0 0.0 collective-permute-done
  18.1 1.3 collective-permute-start.2
  19.4 0.0 collective-permute-done.6
  19.4 1.9 %collective-permute-start.1 = (f32[128,256]{1,0:T(8,128)S(1)}, f32[128,256]{1,0:T(8,128)}, u32[]{:S(2)}, u32[]{:S(2)}) collective-permute-start(f32[128,256]{1,0:T(8,128)S(1)} %get-tuple-element.8), channel_id=1, source_target_pairs={{0,4},{1,5},{16,20},{17,21},{32,36},{33,37},{48,52},{49,53},{64,68... | collective-permute-start | bytes 393224 | tf_op jit(solution)/shard_map/ppermute | solution.py:247
  21.3 0.0 copy-start.1
  21.3 0.0 collective-permute-done.5
  21.3 0.6 collective-permute-done.4
  21.9 0.0 collective-permute-done.3
  21.9 1.1 collective-permute-done.2
  23.0 2.8 %collective-permute-done.1 = f32[128,256]{1,0:T(8,128)} collective-permute-done((f32[128,256]{1,0:T(8,128)S(1)}, f32[128,256]{1,0:T(8,128)}, u32[]{:S(2)}, u32[]{:S(2)}) %collective-permute-start.1) | collective-permute-done | bytes 131104 | tf_op jit(solution)/shard_map/ppermute | solution.py:247
  25.8 1.0 add_add_fusion
  26.8 0.1 broadcast_in_dim.17
  26.9 30.3 %all_to_all.30 = f32[8,128,256]{2,1,0:T(8,128)S(1)} all-to-all(f32[8,128,256]{2,1,0:T(8,128)S(1)} %broadcast_in_dim.17), channel_id=1, replica_groups={{0,2,4,6,8,10,12,14},{1,3,5,7,9,11,13,15},{16,18,20,22,24,26,28,30},{17..., dimensions={0} | all-to-all | bytes 2097152 | tf_op jit(solution)/shard_map/all_to_all | solution.py:223
  57.2 0.0 copy-start
  57.2 5.6 %collective-permute-start.7 = (f32[1024,256]{1,0:T(8,128)S(1)}, f32[1024,256]{1,0:T(8,128)S(1)}, u32[]{:S(2)}, u32[]{:S(2)}) collective-permute-start(f32[1024,256]{1,0:T(8,128)S(1)} %bitcast.6), channel_id=1, source_target_pairs={{0,1},{1,0},{2,3},{3,2},{4,5},{5,4},{6,7},{7,6},{8,9},{9,8},{10,11... | collective-permute-start | bytes 3145736 | tf_op jit(solution)/shard_map/ppermute | solution.py:252
  62.8 2.3 %collective-permute-done.7.other_ref = f32[1024,256]{1,0:T(8,128)S(1)} collective-permute-done((f32[1024,256]{1,0:T(8,128)S(1)}, f32[1024,256]{1,0:T(8,128)S(1)}, u32[]{:S(2)}, u32[]{:S(2)}) %collective-permute-start.7) | collective-permute-done | bytes 1048608 | tf_op jit(solution)/shard_map/ppermute | solution.py:252
  65.1 0.0 copy-start.2
  65.1 0.0 copy-done.1
  65.1 3.6 %shard_map.30 = f32[4,144,512]{2,1,0:T(8,128)S(1)} custom-call(s32[1]{0:T(128)} %bitcast.column_ref, f32[1024,512]{1,0:T(8,128)S(1)} %copy-done.1, f32[1024,256]{1,0:T(8,128)S(1)} %bitcast.7, f32[1024,256]{1,0:T(8,128)S(1)} %collective-permute-done.7.other_ref), custom_call_target="tpu_custom_call" | custom-call | flops 4294967296 | bytes 8388608 | tf_op jit(solution)/shard_map/pallas_call | solution.py:181
  68.7 0.0 copy-done
  68.7 0.0 copy-done.2
  68.7 19.5 %all_to_all.31 = f32[4,144,512]{2,1,0:T(8,128)S(1)} all-to-all(f32[4,144,512]{2,1,0:T(8,128)S(1)} %shard_map.30), channel_id=1, replica_groups={{0,16,32,48},{64,80,96,112},{128,144,160,176},{192,208,224,240},{256,27..., dimensions={0} | all-to-all | bytes 2359296 | tf_op jit(solution)/shard_map/all_to_all | solution.py:223
  88.2 0.1 reduce_sum.18
  88.4 18.3 %all_to_all.32 = f32[8,24,512]{2,1,0:T(8,128)S(1)} all-to-all(f32[8,24,512]{2,1,0:T(8,128)S(1)} %pad_maximum_fusion), channel_id=1, replica_groups={{0,64,128,192,256,320,384,448},{16,80,144,208,272,336,400,464},{32,96,1..., dimensions={0} | all-to-all | bytes 786432 | tf_op jit(solution)/shard_map/all_to_all | solution.py:223
  106.7 0.7 broadcast_in_dim.19
  107.4 3.4 %all-to-all-start.3 = ((f32[8,8,512]{2,1,0:T(8,128)}), f32[8,8,512]{2,1,0:T(8,128)S(1)}, u32[]{:S(2)}, u32[]{:S(2)}) async-start(f32[8,8,512]{2,1,0:T(8,128)} %broadcast_in_dim.19), calls=%async_computation.3 | async-start | bytes 262144 | tf_op jit(solution)/shard_map/all_to_all | solution.py:223
  110.8 7.8 %all-to-all-done.3 = f32[8,8,512]{2,1,0:T(8,128)S(1)} async-done(((f32[8,8,512]{2,1,0:T(8,128)}), f32[8,8,512]{2,1,0:T(8,128)S(1)}, u32[]{:S(2)}, u32[]{:S(2)}) %all-to-all-start.3) | async-done | bytes 131104 | tf_op jit(solution)/shard_map/all_to_all | solution.py:223
  118.6 0.1 broadcast_in_dim.20
  118.7 10.0 %all_to_all.33 = f32[4,80,512]{2,1,0:T(8,128)S(1)} all-to-all(f32[4,80,512]{2,1,0:T(8,128)S(1)} %broadcast_in_dim.20), channel_id=1, replica_groups={{0,16,32,48},{64,80,96,112},{128,144,160,176},{192,208,224,240},{256,27..., dimensions={0} | all-to-all | bytes 1310720 | tf_op jit(solution)/shard_map/all_to_all | solution.py:223
  128.8 8.2 %collective-permute-start.8 = (f32[4,64,512]{2,1,0:T(8,128)S(1)}, f32[4,64,512]{2,1,0:T(8,128)S(1)}, u32[]{:S(2)}, u32[]{:S(2)}) collective-permute-start(f32[4,64,512]{2,1,0:T(8,128)S(1)} %slice.69.gram_ref), channel_id=1, source_target_pairs={{0,1},{1,0},{2,3},{3,2},{4,5},{5,4},{6,7},{7,6},{8,9},{9,8},{10,11... | collective-permute-start | bytes 1572872 | tf_op jit(solution)/shard_map/ppermute | solution.py:274
  137.0 1.1 broadcast_in_dim.41
  138.1 3.7 %all-to-all-start.5 = ((f32[8,64,512]{2,1,0:T(8,128)}), f32[8,64,512]{2,1,0:T(8,128)S(1)}, u32[]{:S(2)}, u32[]{:S(2)}) async-start(f32[8,64,512]{2,1,0:T(8,128)} %broadcast_in_dim.41), calls=%async_computation.5 | async-start | bytes 2097152 | tf_op jit(solution)/shard_map/all_to_all | solution.py:223
  141.8 0.0 collective-permute-done.8.pair_ref
  141.9 20.8 %shard_map.31.inverse_ref = f32[512,512]{1,0:T(8,128)S(1)} custom-call(s32[1]{0:T(128)S(6)} %select_n.22.core_ref, f32[4,64,512]{2,1,0:T(8,128)S(1)} %slice.69.gram_ref, f32[4,64,512]{2,1,0:T(8,128)S(1)} %collective-permute-done.8.pair_ref), custom_call_target="tpu_custom_call" | custom-call | flops 21474836480 | bytes 8388608 | tf_op jit(solution)/shard_map/pallas_call | solution.py:181
  162.7 0.0 copy-start.3
  162.7 1.0 copy-done.3
  163.7 7.2 %all-to-all-done.5 = f32[8,64,512]{2,1,0:T(8,128)S(1)} async-done(((f32[8,64,512]{2,1,0:T(8,128)}), f32[8,64,512]{2,1,0:T(8,128)S(1)}, u32[]{:S(2)}, u32[]{:S(2)}) %all-to-all-start.5) | async-done | bytes 1048608 | tf_op jit(solution)/shard_map/all_to_all | solution.py:223
  170.9 0.0 copy-start.4
  170.9 1.0 copy-done.4
  171.9 7.9 %shard_map.32 = (f32[1024,512]{1,0:T(8,128)}, f32[512,512]{1,0:T(8,128)}) custom-call(s32[1]{0:T(128)} %bitcast.column_ref, f32[1024,512]{1,0:T(8,128)} %snap_ref.3, f32[1024,256]{1,0:T(8,128)} %bitcast.8, f32[1024,256]{1,0:T(8,128)} %copy-done.2, f32[512,512]{1,0:T(8,128)} %copy-done.3, f32[8,4,16,512]{3,2,1,0:T(8,128)} %bitcast.10), custom_call_target="tpu_custom_call" | custom-call | flops 4294967296 | bytes 8388608 | tf_op jit(solution)/shard_map/pallas_call | solution.py:202
  (11 shorter events, 0.2 us)
Async XLA Ops:
  1.9 16.1 %collective-permute-start = (f32[128,256]{1,0:T(8,128)S(1)}, f32[128,256]{1,0:T(8,128)S(1)}, u32[]{:S(2)}, u32[]{:S(2)}) collective-permute-start(f32[128,256]{1,0:T(8,128)S(1)} %get-tuple-element.2), channel_id=1, source_target_pairs={{0,2},{1,3},{16,18},{17,19},{32,34},{33,35},{48,50},{49,51},{64,66... | collective-permute-start | bytes 393224 | tf_op jit(solution)/shard_map/ppermute | solution.py:247
  6.8 12.6 %collective-permute-start.6 = (f32[128,256]{1,0:T(8,128)S(1)}, f32[128,256]{1,0:T(8,128)S(1)}, u32[]{:S(2)}, u32[]{:S(2)}) collective-permute-start(f32[128,256]{1,0:T(8,128)S(1)} %get-tuple-element.3), channel_id=1, source_target_pairs={{0,14},{1,15},{16,30},{17,31},{32,46},{33,47},{48,62},{49,63},{64,... | collective-permute-start | bytes 393224 | tf_op jit(solution)/shard_map/ppermute | solution.py:247
  14.1 7.2 %collective-permute-start.5 = (f32[128,256]{1,0:T(8,128)S(1)}, f32[128,256]{1,0:T(8,128)S(1)}, u32[]{:S(2)}, u32[]{:S(2)}) collective-permute-start(f32[128,256]{1,0:T(8,128)S(1)} %get-tuple-element.4), channel_id=1, source_target_pairs={{0,12},{1,13},{16,28},{17,29},{32,44},{33,45},{48,60},{49,61},{64,... | collective-permute-start | bytes 393224 | tf_op jit(solution)/shard_map/ppermute | solution.py:247
  15.4 6.5 %collective-permute-start.4 = (f32[128,256]{1,0:T(8,128)S(1)}, f32[128,256]{1,0:T(8,128)S(1)}, u32[]{:S(2)}, u32[]{:S(2)}) collective-permute-start(f32[128,256]{1,0:T(8,128)S(1)} %get-tuple-element.5), channel_id=1, source_target_pairs={{0,10},{1,11},{16,26},{17,27},{32,42},{33,43},{48,58},{49,59},{64,... | collective-permute-start | bytes 393224 | tf_op jit(solution)/shard_map/ppermute | solution.py:247
  16.7 5.2 %collective-permute-start.3 = (f32[128,256]{1,0:T(8,128)S(1)}, f32[128,256]{1,0:T(8,128)S(1)}, u32[]{:S(2)}, u32[]{:S(2)}) collective-permute-start(f32[128,256]{1,0:T(8,128)S(1)} %get-tuple-element.6), channel_id=1, source_target_pairs={{0,8},{1,9},{16,24},{17,25},{32,40},{33,41},{48,56},{49,57},{64,72... | collective-permute-start | bytes 393224 | tf_op jit(solution)/shard_map/ppermute | solution.py:247
  18.1 4.9 %collective-permute-start.2 = (f32[128,256]{1,0:T(8,128)S(1)}, f32[128,256]{1,0:T(8,128)S(1)}, u32[]{:S(2)}, u32[]{:S(2)}) collective-permute-start(f32[128,256]{1,0:T(8,128)S(1)} %get-tuple-element.7), channel_id=1, source_target_pairs={{0,6},{1,7},{16,22},{17,23},{32,38},{33,39},{48,54},{49,55},{64,70... | collective-permute-start | bytes 393224 | tf_op jit(solution)/shard_map/ppermute | solution.py:247
  19.4 6.4 %collective-permute-start.1 = (f32[128,256]{1,0:T(8,128)S(1)}, f32[128,256]{1,0:T(8,128)}, u32[]{:S(2)}, u32[]{:S(2)}) collective-permute-start(f32[128,256]{1,0:T(8,128)S(1)} %get-tuple-element.8), channel_id=1, source_target_pairs={{0,4},{1,5},{16,20},{17,21},{32,36},{33,37},{48,52},{49,53},{64,68... | collective-permute-start | bytes 393224 | tf_op jit(solution)/shard_map/ppermute | solution.py:247
  21.3 43.8 %copy-start.1 = (f32[1024,512]{1,0:T(8,128)S(1)}, f32[1024,512]{1,0:T(8,128)}, u32[]{:S(2)}) copy-start(f32[1024,512]{1,0:T(8,128)} %snap_ref.3) | copy-start | bytes 6291460
  57.2 11.5 %copy-start = (f32[8,128,256]{2,1,0:T(8,128)}, f32[8,128,256]{2,1,0:T(8,128)S(1)}, u32[]{:S(2)}) copy-start(f32[8,128,256]{2,1,0:T(8,128)S(1)} %all_to_all.30) | copy-start | bytes 3145732
  57.2 7.9 %collective-permute-start.7 = (f32[1024,256]{1,0:T(8,128)S(1)}, f32[1024,256]{1,0:T(8,128)S(1)}, u32[]{:S(2)}, u32[]{:S(2)}) collective-permute-start(f32[1024,256]{1,0:T(8,128)S(1)} %bitcast.6), channel_id=1, source_target_pairs={{0,1},{1,0},{2,3},{3,2},{4,5},{5,4},{6,7},{7,6},{8,9},{9,8},{10,11... | collective-permute-start | bytes 3145736 | tf_op jit(solution)/shard_map/ppermute | solution.py:252
  65.1 3.6 %copy-start.2 = (f32[1024,256]{1,0:T(8,128)}, f32[1024,256]{1,0:T(8,128)S(1)}, u32[]{:S(2)}) copy-start(f32[1024,256]{1,0:T(8,128)S(1)} %collective-permute-done.7.other_ref) | copy-start | bytes 3145732
  107.4 11.2 %all-to-all-start.3 = ((f32[8,8,512]{2,1,0:T(8,128)}), f32[8,8,512]{2,1,0:T(8,128)S(1)}, u32[]{:S(2)}, u32[]{:S(2)}) async-start(f32[8,8,512]{2,1,0:T(8,128)} %broadcast_in_dim.19), calls=%async_computation.3 | async-start | bytes 262144 | tf_op jit(solution)/shard_map/all_to_all | solution.py:223
  128.8 13.1 %collective-permute-start.8 = (f32[4,64,512]{2,1,0:T(8,128)S(1)}, f32[4,64,512]{2,1,0:T(8,128)S(1)}, u32[]{:S(2)}, u32[]{:S(2)}) collective-permute-start(f32[4,64,512]{2,1,0:T(8,128)S(1)} %slice.69.gram_ref), channel_id=1, source_target_pairs={{0,1},{1,0},{2,3},{3,2},{4,5},{5,4},{6,7},{7,6},{8,9},{9,8},{10,11... | collective-permute-start | bytes 1572872 | tf_op jit(solution)/shard_map/ppermute | solution.py:274
  138.1 32.8 %all-to-all-start.5 = ((f32[8,64,512]{2,1,0:T(8,128)}), f32[8,64,512]{2,1,0:T(8,128)S(1)}, u32[]{:S(2)}, u32[]{:S(2)}) async-start(f32[8,64,512]{2,1,0:T(8,128)} %broadcast_in_dim.41), calls=%async_computation.5 | async-start | bytes 2097152 | tf_op jit(solution)/shard_map/all_to_all | solution.py:223
  162.7 1.0 copy-start.3
  170.9 1.0 copy-start.4

commit v3 on v2

--- a/solution.py
+++ b/solution.py
@@ -270,7 +270,7 @@
         factor_kernel,
         [(2 * NB, 2 * NB)],
         [(2 * NB, 2 * NB)],
-        20 << 30,
+        1 << 30,
         place % 2, gram, lax.ppermute(gram, "col", swap),
     )
     factored, upper = finish(

time: 180 us -> 175 us (0.972)
  waiting for transfers between devices: 21.8 us -> 15.9 us
    all_to_all x2, waiting for transfers between devices: 15 us -> 7.82 us  [trade(): return lax.all_to_all(parts, axis, 0, 0, axis_index_groups=groups)]
  transfers between devices with their start and end apart: 11 -> 11, of which waited for: 6 -> 6; matrix products, arithmetic and copies ran while one was open for 1% -> 0% of each run, Pallas kernels for 12% -> 12%
where the time goes in v3:
time: 175 us; the launch traced here: 174 us
  blocking collectives  78 us (45%)
  starting transfers between devices  40.2 us (23%)
  Pallas kernels  32.4 us (19%)
  waiting for transfers between devices  15.9 us (9%)
  local copies, waits for them, and re-layouts  5.28 us (3%)
    all_to_all x4, blocking collectives, trade(): return lax.all_to_all(parts, axis, 0, 0, axis_index_groups=groups)  78 us
    pallas_call x2, Pallas kernels, call(): pl.pallas_call(kernel, out_shape=[jax.ShapeDtypeStruct(s, jnp.float32) fo...  24.5 us
    ppermute x7, starting transfers between devices, body(): lax.ppermute(mine[k * step:(k + 1) * step], 'col', [(c, 2 * k + c) for c...  19.3 us
    all_to_all x2, starting transfers between devices, trade(): return lax.all_to_all(parts, axis, 0, 0, axis_index_groups=groups)  8.37 us
    pallas_call x1, Pallas kernels, finish(): pl.pallas_call(finish_kernel, grid=(rows // tile,), out_shape=[jax.ShapeD...  7.94 us
    all_to_all x2, waiting for transfers between devices, trade(): return lax.all_to_all(parts, axis, 0, 0, axis_index_groups=groups)  7.82 us
    ppermute x1, starting transfers between devices, body(): lax.ppermute(gram, 'col', swap)  6.97 us
    ppermute x1, starting transfers between devices, body(): other = lax.ppermute(panel, 'col', swap)  5.59 us
  transfers between devices with their start and end apart: 11, of which 6 were waited for; matrix products, arithmetic and copies ran while one was open for 0% of the time, Pallas kernels for 12%

profile of v3, /device:TPU:1, one launch (start us, length us, event | category | flops | bytes accessed | tf_op | source)
XLA Modules:
  0.0 173.9 jit_solution(7088679172188699770)
XLA Ops:
  0.6 1.3 fusion
  1.9 4.8 %collective-permute-start = (f32[128,256]{1,0:T(8,128)S(1)}, f32[128,256]{1,0:T(8,128)S(1)}, u32[]{:S(2)}, u32[]{:S(2)}) collective-permute-start(f32[128,256]{1,0:T(8,128)S(1)} %get-tuple-element.2), channel_id=1, source_target_pairs={{0,2},{1,3},{16,18},{17,19},{32,34},{33,35},{48,50},{49,51},{64,66... | collective-permute-start | bytes 393224 | tf_op jit(solution)/shard_map/ppermute | solution.py:247
  6.8 7.3 %collective-permute-start.6 = (f32[128,256]{1,0:T(8,128)S(1)}, f32[128,256]{1,0:T(8,128)S(1)}, u32[]{:S(2)}, u32[]{:S(2)}) collective-permute-start(f32[128,256]{1,0:T(8,128)S(1)} %get-tuple-element.3), channel_id=1, source_target_pairs={{0,14},{1,15},{16,30},{17,31},{32,46},{33,47},{48,62},{49,63},{64,... | collective-permute-start | bytes 393224 | tf_op jit(solution)/shard_map/ppermute | solution.py:247
  14.1 1.3 collective-permute-start.5
  15.4 1.3 collective-permute-start.4
  16.7 1.3 collective-permute-start.3
  18.0 0.0 collective-permute-done
  18.1 1.3 collective-permute-start.2
  19.4 0.0 collective-permute-done.6
  19.4 1.9 %collective-permute-start.1 = (f32[128,256]{1,0:T(8,128)S(1)}, f32[128,256]{1,0:T(8,128)}, u32[]{:S(2)}, u32[]{:S(2)}) collective-permute-start(f32[128,256]{1,0:T(8,128)S(1)} %get-tuple-element.8), channel_id=1, source_target_pairs={{0,4},{1,5},{16,20},{17,21},{32,36},{33,37},{48,52},{49,53},{64,68... | collective-permute-start | bytes 393224 | tf_op jit(solution)/shard_map/ppermute | solution.py:247
  21.3 0.0 copy-start.1
  21.3 0.0 collective-permute-done.5
  21.3 0.6 collective-permute-done.4
  21.9 0.0 collective-permute-done.3
  21.9 1.1 collective-permute-done.2
  23.0 2.8 %collective-permute-done.1 = f32[128,256]{1,0:T(8,128)} collective-permute-done((f32[128,256]{1,0:T(8,128)S(1)}, f32[128,256]{1,0:T(8,128)}, u32[]{:S(2)}, u32[]{:S(2)}) %collective-permute-start.1) | collective-permute-done | bytes 131104 | tf_op jit(solution)/shard_map/ppermute | solution.py:247
  25.8 1.0 add_add_fusion
  26.8 0.1 broadcast_in_dim.17
  26.9 30.3 %all_to_all.30 = f32[8,128,256]{2,1,0:T(8,128)S(1)} all-to-all(f32[8,128,256]{2,1,0:T(8,128)S(1)} %broadcast_in_dim.17), channel_id=1, replica_groups={{0,2,4,6,8,10,12,14},{1,3,5,7,9,11,13,15},{16,18,20,22,24,26,28,30},{17..., dimensions={0} | all-to-all | bytes 2097152 | tf_op jit(solution)/shard_map/all_to_all | solution.py:223
  57.2 0.0 copy-start
  57.2 5.6 %collective-permute-start.7 = (f32[1024,256]{1,0:T(8,128)S(1)}, f32[1024,256]{1,0:T(8,128)S(1)}, u32[]{:S(2)}, u32[]{:S(2)}) collective-permute-start(f32[1024,256]{1,0:T(8,128)S(1)} %bitcast.6), channel_id=1, source_target_pairs={{0,1},{1,0},{2,3},{3,2},{4,5},{5,4},{6,7},{7,6},{8,9},{9,8},{10,11... | collective-permute-start | bytes 3145736 | tf_op jit(solution)/shard_map/ppermute | solution.py:252
  62.8 2.3 %collective-permute-done.7.other_ref = f32[1024,256]{1,0:T(8,128)S(1)} collective-permute-done((f32[1024,256]{1,0:T(8,128)S(1)}, f32[1024,256]{1,0:T(8,128)S(1)}, u32[]{:S(2)}, u32[]{:S(2)}) %collective-permute-start.7) | collective-permute-done | bytes 1048608 | tf_op jit(solution)/shard_map/ppermute | solution.py:252
  65.1 0.0 copy-start.2
  65.1 0.0 copy-done.1
  65.1 3.6 %shard_map.30 = f32[4,144,512]{2,1,0:T(8,128)S(1)} custom-call(s32[1]{0:T(128)} %bitcast.column_ref, f32[1024,512]{1,0:T(8,128)S(1)} %copy-done.1, f32[1024,256]{1,0:T(8,128)S(1)} %bitcast.7, f32[1024,256]{1,0:T(8,128)S(1)} %collective-permute-done.7.other_ref), custom_call_target="tpu_custom_call" | custom-call | flops 4294967296 | bytes 8388608 | tf_op jit(solution)/shard_map/pallas_call | solution.py:181
  68.7 0.0 copy-done
  68.7 0.0 copy-done.2
  68.7 19.5 %all_to_all.31 = f32[4,144,512]{2,1,0:T(8,128)S(1)} all-to-all(f32[4,144,512]{2,1,0:T(8,128)S(1)} %shard_map.30), channel_id=1, replica_groups={{0,16,32,48},{64,80,96,112},{128,144,160,176},{192,208,224,240},{256,27..., dimensions={0} | all-to-all | bytes 2359296 | tf_op jit(solution)/shard_map/all_to_all | solution.py:223
  88.2 0.1 reduce_sum.18
  88.4 18.3 %all_to_all.32 = f32[8,24,512]{2,1,0:T(8,128)S(1)} all-to-all(f32[8,24,512]{2,1,0:T(8,128)S(1)} %pad_maximum_fusion), channel_id=1, replica_groups={{0,64,128,192,256,320,384,448},{16,80,144,208,272,336,400,464},{32,96,1..., dimensions={0} | all-to-all | bytes 786432 | tf_op jit(solution)/shard_map/all_to_all | solution.py:223
  106.7 0.7 broadcast_in_dim.19
  107.4 3.4 %all-to-all-start.3 = ((f32[8,8,512]{2,1,0:T(8,128)}), f32[8,8,512]{2,1,0:T(8,128)S(1)}, u32[]{:S(2)}, u32[]{:S(2)}) async-start(f32[8,8,512]{2,1,0:T(8,128)} %broadcast_in_dim.19), calls=%async_computation.3 | async-start | bytes 262144 | tf_op jit(solution)/shard_map/all_to_all | solution.py:223
  110.8 7.8 %all-to-all-done.3 = f32[8,8,512]{2,1,0:T(8,128)S(1)} async-done(((f32[8,8,512]{2,1,0:T(8,128)}), f32[8,8,512]{2,1,0:T(8,128)S(1)}, u32[]{:S(2)}, u32[]{:S(2)}) %all-to-all-start.3) | async-done | bytes 131104 | tf_op jit(solution)/shard_map/all_to_all | solution.py:223
  118.6 0.1 broadcast_in_dim.20
  118.7 10.0 %all_to_all.33 = f32[4,80,512]{2,1,0:T(8,128)S(1)} all-to-all(f32[4,80,512]{2,1,0:T(8,128)S(1)} %broadcast_in_dim.20), channel_id=1, replica_groups={{0,16,32,48},{64,80,96,112},{128,144,160,176},{192,208,224,240},{256,27..., dimensions={0} | all-to-all | bytes 1310720 | tf_op jit(solution)/shard_map/all_to_all | solution.py:223
  128.7 1.1 broadcast_in_dim.41
  129.8 5.0 %all-to-all-start.5 = ((f32[8,64,512]{2,1,0:T(8,128)}), f32[8,64,512]{2,1,0:T(8,128)S(1)}, u32[]{:S(2)}, u32[]{:S(2)}) async-start(f32[8,64,512]{2,1,0:T(8,128)} %broadcast_in_dim.41), calls=%async_computation.5 | async-start | bytes 2097152 | tf_op jit(solution)/shard_map/all_to_all | solution.py:223
  134.9 7.0 %collective-permute-start.8 = (f32[4,64,512]{2,1,0:T(8,128)S(1)}, f32[4,64,512]{2,1,0:T(8,128)S(1)}, u32[]{:S(2)}, u32[]{:S(2)}) collective-permute-start(f32[4,64,512]{2,1,0:T(8,128)S(1)} %slice.69.gram_ref), channel_id=1, source_target_pairs={{0,1},{1,0},{2,3},{3,2},{4,5},{5,4},{6,7},{7,6},{8,9},{9,8},{10,11... | collective-permute-start | bytes 1572872 | tf_op jit(solution)/shard_map/ppermute | solution.py:274
  141.8 1.3 collective-permute-done.8.pair_ref
  143.2 20.8 %shard_map.31.inverse_ref = f32[512,512]{1,0:T(8,128)S(1)} custom-call(s32[1]{0:T(128)S(6)} %select_n.22.core_ref, f32[4,64,512]{2,1,0:T(8,128)S(1)} %slice.69.gram_ref, f32[4,64,512]{2,1,0:T(8,128)S(1)} %collective-permute-done.8.pair_ref), custom_call_target="tpu_custom_call" | custom-call | flops 1073741824 | bytes 8388608 | tf_op jit(solution)/shard_map/pallas_call | solution.py:181
  164.0 0.0 copy-start.3
  164.0 1.0 copy-done.3
  165.0 0.0 all-to-all-done.5
  165.0 0.0 copy-start.4
  165.0 1.0 copy-done.4
  166.0 7.9 %shard_map.32 = (f32[1024,512]{1,0:T(8,128)}, f32[512,512]{1,0:T(8,128)}) custom-call(s32[1]{0:T(128)} %bitcast.column_ref, f32[1024,512]{1,0:T(8,128)} %snap_ref.3, f32[1024,256]{1,0:T(8,128)} %bitcast.8, f32[1024,256]{1,0:T(8,128)} %copy-done.2, f32[512,512]{1,0:T(8,128)} %copy-done.3, f32[8,4,16,512]{3,2,1,0:T(8,128)} %bitcast.10), custom_call_target="tpu_custom_call" | custom-call | flops 4294967296 | bytes 8388608 | tf_op jit(solution)/shard_map/pallas_call | solution.py:202
  (11 shorter events, 0.2 us)
Async XLA Ops:
  1.9 16.1 %collective-permute-start = (f32[128,256]{1,0:T(8,128)S(1)}, f32[128,256]{1,0:T(8,128)S(1)}, u32[]{:S(2)}, u32[]{:S(2)}) collective-permute-start(f32[128,256]{1,0:T(8,128)S(1)} %get-tuple-element.2), channel_id=1, source_target_pairs={{0,2},{1,3},{16,18},{17,19},{32,34},{33,35},{48,50},{49,51},{64,66... | collective-permute-start | bytes 393224 | tf_op jit(solution)/shard_map/ppermute | solution.py:247
  6.8 12.6 %collective-permute-start.6 = (f32[128,256]{1,0:T(8,128)S(1)}, f32[128,256]{1,0:T(8,128)S(1)}, u32[]{:S(2)}, u32[]{:S(2)}) collective-permute-start(f32[128,256]{1,0:T(8,128)S(1)} %get-tuple-element.3), channel_id=1, source_target_pairs={{0,14},{1,15},{16,30},{17,31},{32,46},{33,47},{48,62},{49,63},{64,... | collective-permute-start | bytes 393224 | tf_op jit(solution)/shard_map/ppermute | solution.py:247
  14.1 7.2 %collective-permute-start.5 = (f32[128,256]{1,0:T(8,128)S(1)}, f32[128,256]{1,0:T(8,128)S(1)}, u32[]{:S(2)}, u32[]{:S(2)}) collective-permute-start(f32[128,256]{1,0:T(8,128)S(1)} %get-tuple-element.4), channel_id=1, source_target_pairs={{0,12},{1,13},{16,28},{17,29},{32,44},{33,45},{48,60},{49,61},{64,... | collective-permute-start | bytes 393224 | tf_op jit(solution)/shard_map/ppermute | solution.py:247
  15.4 6.5 %collective-permute-start.4 = (f32[128,256]{1,0:T(8,128)S(1)}, f32[128,256]{1,0:T(8,128)S(1)}, u32[]{:S(2)}, u32[]{:S(2)}) collective-permute-start(f32[128,256]{1,0:T(8,128)S(1)} %get-tuple-element.5), channel_id=1, source_target_pairs={{0,10},{1,11},{16,26},{17,27},{32,42},{33,43},{48,58},{49,59},{64,... | collective-permute-start | bytes 393224 | tf_op jit(solution)/shard_map/ppermute | solution.py:247
  16.7 5.2 %collective-permute-start.3 = (f32[128,256]{1,0:T(8,128)S(1)}, f32[128,256]{1,0:T(8,128)S(1)}, u32[]{:S(2)}, u32[]{:S(2)}) collective-permute-start(f32[128,256]{1,0:T(8,128)S(1)} %get-tuple-element.6), channel_id=1, source_target_pairs={{0,8},{1,9},{16,24},{17,25},{32,40},{33,41},{48,56},{49,57},{64,72... | collective-permute-start | bytes 393224 | tf_op jit(solution)/shard_map/ppermute | solution.py:247
  18.1 4.9 %collective-permute-start.2 = (f32[128,256]{1,0:T(8,128)S(1)}, f32[128,256]{1,0:T(8,128)S(1)}, u32[]{:S(2)}, u32[]{:S(2)}) collective-permute-start(f32[128,256]{1,0:T(8,128)S(1)} %get-tuple-element.7), channel_id=1, source_target_pairs={{0,6},{1,7},{16,22},{17,23},{32,38},{33,39},{48,54},{49,55},{64,70... | collective-permute-start | bytes 393224 | tf_op jit(solution)/shard_map/ppermute | solution.py:247
  19.4 6.4 %collective-permute-start.1 = (f32[128,256]{1,0:T(8,128)S(1)}, f32[128,256]{1,0:T(8,128)}, u32[]{:S(2)}, u32[]{:S(2)}) collective-permute-start(f32[128,256]{1,0:T(8,128)S(1)} %get-tuple-element.8), channel_id=1, source_target_pairs={{0,4},{1,5},{16,20},{17,21},{32,36},{33,37},{48,52},{49,53},{64,68... | collective-permute-start | bytes 393224 | tf_op jit(solution)/shard_map/ppermute | solution.py:247
  21.3 43.8 %copy-start.1 = (f32[1024,512]{1,0:T(8,128)S(1)}, f32[1024,512]{1,0:T(8,128)}, u32[]{:S(2)}) copy-start(f32[1024,512]{1,0:T(8,128)} %snap_ref.3) | copy-start | bytes 6291460
  57.2 11.5 %copy-start = (f32[8,128,256]{2,1,0:T(8,128)}, f32[8,128,256]{2,1,0:T(8,128)S(1)}, u32[]{:S(2)}) copy-start(f32[8,128,256]{2,1,0:T(8,128)S(1)} %all_to_all.30) | copy-start | bytes 3145732
  57.2 7.9 %collective-permute-start.7 = (f32[1024,256]{1,0:T(8,128)S(1)}, f32[1024,256]{1,0:T(8,128)S(1)}, u32[]{:S(2)}, u32[]{:S(2)}) collective-permute-start(f32[1024,256]{1,0:T(8,128)S(1)} %bitcast.6), channel_id=1, source_target_pairs={{0,1},{1,0},{2,3},{3,2},{4,5},{5,4},{6,7},{7,6},{8,9},{9,8},{10,11... | collective-permute-start | bytes 3145736 | tf_op jit(solution)/shard_map/ppermute | solution.py:252
  65.1 3.6 %copy-start.2 = (f32[1024,256]{1,0:T(8,128)}, f32[1024,256]{1,0:T(8,128)S(1)}, u32[]{:S(2)}) copy-start(f32[1024,256]{1,0:T(8,128)S(1)} %collective-permute-done.7.other_ref) | copy-start | bytes 3145732
  107.4 11.2 %all-to-all-start.3 = ((f32[8,8,512]{2,1,0:T(8,128)}), f32[8,8,512]{2,1,0:T(8,128)S(1)}, u32[]{:S(2)}, u32[]{:S(2)}) async-start(f32[8,8,512]{2,1,0:T(8,128)} %broadcast_in_dim.19), calls=%async_computation.3 | async-start | bytes 262144 | tf_op jit(solution)/shard_map/all_to_all | solution.py:223
  129.8 35.2 %all-to-all-start.5 = ((f32[8,64,512]{2,1,0:T(8,128)}), f32[8,64,512]{2,1,0:T(8,128)S(1)}, u32[]{:S(2)}, u32[]{:S(2)}) async-start(f32[8,64,512]{2,1,0:T(8,128)} %broadcast_in_dim.41), calls=%async_computation.5 | async-start | bytes 2097152 | tf_op jit(solution)/shard_map/all_to_all | solution.py:223
  134.9 8.3 %collective-permute-start.8 = (f32[4,64,512]{2,1,0:T(8,128)S(1)}, f32[4,64,512]{2,1,0:T(8,128)S(1)}, u32[]{:S(2)}, u32[]{:S(2)}) collective-permute-start(f32[4,64,512]{2,1,0:T(8,128)S(1)} %slice.69.gram_ref), channel_id=1, source_target_pairs={{0,1},{1,0},{2,3},{3,2},{4,5},{5,4},{6,7},{7,6},{8,9},{9,8},{10,11... | collective-permute-start | bytes 1572872 | tf_op jit(solution)/shard_map/ppermute | solution.py:274
  164.0 1.0 copy-start.3
  165.0 1.0 copy-start.4

commit v4 on v3

--- a/solution.py
+++ b/solution.py
@@ -102,7 +102,7 @@
 def inner_kernel(column_ref, snap_ref, panel_ref, other_ref, out_ref, gram_ref):
     column = column_ref[0]
     even, z = column % 2 == 0, column // 2
-    nx, tall, width = out_ref.shape
+    nx, _, width = out_ref.shape
     cut = 2 * NB // nx
     mine, other = panel_ref[...], other_ref[...]
     snap = split(snap_ref[...])
@@ -117,7 +117,6 @@
         rows = pl.ds(pl.multiple_of(x * (NB // nx) + z * 8, 8), 8)
         out_ref[x, cut:cut + 8, :3 * BLK] = gram_ref[rows, :]
         out_ref[x, cut:cut + 8, 3 * BLK:] = jnp.zeros((8, width - 3 * BLK), jnp.float32)
-        out_ref[x, cut + 8:, :] = jnp.zeros((tall - cut - 8, width), jnp.float32)
 
 
 def factor_kernel(core_ref, gram_ref, pair_ref, inverse_ref, s_ref):
@@ -191,7 +190,7 @@
 
 def finish(column, snapshots, panel, other, inverse, inner):
     rows, width = snapshots.shape
-    tile = 256
+    tile = 512
 
     def whole(shape):
         return pl.BlockSpec(shape, lambda i: (0,) * len(shape))
@@ -254,7 +253,7 @@
     place = column.astype(jnp.int32).reshape(1)
     cut = 2 * NB // nx
     inner, = call(
-        inner_kernel, [(nx, cut + 16, width)], [(NB, 3 * BLK)], 4 << 30, place, snapshots, panel, other
+        inner_kernel, [(nx, cut + 8, width)], [(NB, 3 * BLK)], 4 << 30, place, snapshots, panel, other
     )
     sums = jnp.sum(trade(inner, "row", x_groups), axis=0) * scale
     inner = sums[:cut].reshape(ny, cut // ny, width)

time: 175 us -> 174 us (level)
  no operation moved by 1% of the time
where the time goes in v4:
time: 174 us; the launch traced here: 173 us
  blocking collectives  78.3 us (45%)
  starting transfers between devices  39.4 us (23%)
  Pallas kernels  32 us (18%)
  waiting for transfers between devices  16 us (9%)
  local copies, waits for them, and re-layouts  5.28 us (3%)
    all_to_all x4, blocking collectives, trade(): return lax.all_to_all(parts, axis, 0, 0, axis_index_groups=groups)  78.3 us
    pallas_call x2, Pallas kernels, call(): pl.pallas_call(kernel, out_shape=[jax.ShapeDtypeStruct(s, jnp.float32) fo...  24.5 us
    ppermute x7, starting transfers between devices, body(): lax.ppermute(mine[k * step:(k + 1) * step], 'col', [(c, 2 * k + c) for c...  19.3 us
    all_to_all x2, waiting for transfers between devices, trade(): return lax.all_to_all(parts, axis, 0, 0, axis_index_groups=groups)  7.93 us
    pallas_call x1, Pallas kernels, finish(): pl.pallas_call(finish_kernel, grid=(rows // tile,), out_shape=[jax.ShapeD...  7.54 us
    all_to_all x2, starting transfers between devices, trade(): return lax.all_to_all(parts, axis, 0, 0, axis_index_groups=groups)  7.42 us
    ppermute x1, starting transfers between devices, body(): lax.ppermute(gram, 'col', swap)  7.08 us
    ppermute x1, starting transfers between devices, body(): other = lax.ppermute(panel, 'col', swap)  5.59 us
  transfers between devices with their start and end apart: 11, of which 6 were waited for; matrix products, arithmetic and copies ran while one was open for 0% of the time, Pallas kernels for 12%

profile of v4, /device:TPU:1, one launch (start us, length us, event | category | flops | bytes accessed | tf_op | source)
XLA Modules:
  0.0 173.1 jit_solution(15795640886499272713)
XLA Ops:
  0.6 1.3 fusion
  1.9 4.8 %collective-permute-start = (f32[128,256]{1,0:T(8,128)S(1)}, f32[128,256]{1,0:T(8,128)S(1)}, u32[]{:S(2)}, u32[]{:S(2)}) collective-permute-start(f32[128,256]{1,0:T(8,128)S(1)} %get-tuple-element.2), channel_id=1, source_target_pairs={{0,2},{1,3},{16,18},{17,19},{32,34},{33,35},{48,50},{49,51},{64,66... | collective-permute-start | bytes 393224 | tf_op jit(solution)/shard_map/ppermute | solution.py:246
  6.8 7.3 %collective-permute-start.6 = (f32[128,256]{1,0:T(8,128)S(1)}, f32[128,256]{1,0:T(8,128)S(1)}, u32[]{:S(2)}, u32[]{:S(2)}) collective-permute-start(f32[128,256]{1,0:T(8,128)S(1)} %get-tuple-element.3), channel_id=1, source_target_pairs={{0,14},{1,15},{16,30},{17,31},{32,46},{33,47},{48,62},{49,63},{64,... | collective-permute-start | bytes 393224 | tf_op jit(solution)/shard_map/ppermute | solution.py:246
  14.1 1.3 collective-permute-start.5
  15.4 1.3 collective-permute-start.4
  16.7 1.3 collective-permute-start.3
  18.0 0.0 collective-permute-done
  18.1 1.3 collective-permute-start.2
  19.4 0.0 collective-permute-done.6
  19.4 1.9 %collective-permute-start.1 = (f32[128,256]{1,0:T(8,128)S(1)}, f32[128,256]{1,0:T(8,128)}, u32[]{:S(2)}, u32[]{:S(2)}) collective-permute-start(f32[128,256]{1,0:T(8,128)S(1)} %get-tuple-element.8), channel_id=1, source_target_pairs={{0,4},{1,5},{16,20},{17,21},{32,36},{33,37},{48,52},{49,53},{64,68... | collective-permute-start | bytes 393224 | tf_op jit(solution)/shard_map/ppermute | solution.py:246
  21.3 0.0 copy-start.1
  21.3 0.0 collective-permute-done.5
  21.3 0.6 collective-permute-done.4
  21.9 0.0 collective-permute-done.3
  21.9 1.1 collective-permute-done.2
  23.0 2.8 %collective-permute-done.1 = f32[128,256]{1,0:T(8,128)} collective-permute-done((f32[128,256]{1,0:T(8,128)S(1)}, f32[128,256]{1,0:T(8,128)}, u32[]{:S(2)}, u32[]{:S(2)}) %collective-permute-start.1) | collective-permute-done | bytes 131104 | tf_op jit(solution)/shard_map/ppermute | solution.py:246
  25.8 1.0 add_add_fusion
  26.8 0.1 broadcast_in_dim.17
  26.9 30.3 %all_to_all.30 = f32[8,128,256]{2,1,0:T(8,128)S(1)} all-to-all(f32[8,128,256]{2,1,0:T(8,128)S(1)} %broadcast_in_dim.17), channel_id=1, replica_groups={{0,2,4,6,8,10,12,14},{1,3,5,7,9,11,13,15},{16,18,20,22,24,26,28,30},{17..., dimensions={0} | all-to-all | bytes 2097152 | tf_op jit(solution)/shard_map/all_to_all | solution.py:222
  57.2 0.0 copy-start
  57.2 5.6 %collective-permute-start.7 = (f32[1024,256]{1,0:T(8,128)S(1)}, f32[1024,256]{1,0:T(8,128)S(1)}, u32[]{:S(2)}, u32[]{:S(2)}) collective-permute-start(f32[1024,256]{1,0:T(8,128)S(1)} %bitcast.6), channel_id=1, source_target_pairs={{0,1},{1,0},{2,3},{3,2},{4,5},{5,4},{6,7},{7,6},{8,9},{9,8},{10,11... | collective-permute-start | bytes 3145736 | tf_op jit(solution)/shard_map/ppermute | solution.py:251
  62.8 2.3 %collective-permute-done.7.other_ref = f32[1024,256]{1,0:T(8,128)S(1)} collective-permute-done((f32[1024,256]{1,0:T(8,128)S(1)}, f32[1024,256]{1,0:T(8,128)S(1)}, u32[]{:S(2)}, u32[]{:S(2)}) %collective-permute-start.7) | collective-permute-done | bytes 1048608 | tf_op jit(solution)/shard_map/ppermute | solution.py:251
  65.1 0.0 copy-start.2
  65.1 0.0 copy-done.1
  65.1 3.6 %shard_map.30 = f32[4,136,512]{2,1,0:T(8,128)S(1)} custom-call(s32[1]{0:T(128)} %bitcast.column_ref, f32[1024,512]{1,0:T(8,128)S(1)} %copy-done.1, f32[1024,256]{1,0:T(8,128)S(1)} %bitcast.7, f32[1024,256]{1,0:T(8,128)S(1)} %collective-permute-done.7.other_ref), custom_call_target="tpu_custom_call" | custom-call | flops 4294967296 | bytes 8388608 | tf_op jit(solution)/shard_map/pallas_call | solution.py:180
  68.7 0.0 copy-done
  68.7 0.0 copy-done.2
  68.7 19.0 %all_to_all.31 = f32[4,136,512]{2,1,0:T(8,128)S(1)} all-to-all(f32[4,136,512]{2,1,0:T(8,128)S(1)} %shard_map.30), channel_id=1, replica_groups={{0,16,32,48},{64,80,96,112},{128,144,160,176},{192,208,224,240},{256,27..., dimensions={0} | all-to-all | bytes 2228224 | tf_op jit(solution)/shard_map/all_to_all | solution.py:222
  87.8 0.1 reduce_sum.18
  88.0 19.0 %all_to_all.32 = f32[8,24,512]{2,1,0:T(8,128)S(1)} all-to-all(f32[8,24,512]{2,1,0:T(8,128)S(1)} %pad_maximum_fusion), channel_id=1, replica_groups={{0,64,128,192,256,320,384,448},{16,80,144,208,272,336,400,464},{32,96,1..., dimensions={0} | all-to-all | bytes 786432 | tf_op jit(solution)/shard_map/all_to_all | solution.py:222
  107.0 0.7 broadcast_in_dim.19
  107.7 3.4 %all-to-all-start.3 = ((f32[8,8,512]{2,1,0:T(8,128)}), f32[8,8,512]{2,1,0:T(8,128)S(1)}, u32[]{:S(2)}, u32[]{:S(2)}) async-start(f32[8,8,512]{2,1,0:T(8,128)} %broadcast_in_dim.19), calls=%async_computation.3 | async-start | bytes 262144 | tf_op jit(solution)/shard_map/all_to_all | solution.py:222
  111.1 7.9 %all-to-all-done.3 = f32[8,8,512]{2,1,0:T(8,128)S(1)} async-done(((f32[8,8,512]{2,1,0:T(8,128)}), f32[8,8,512]{2,1,0:T(8,128)S(1)}, u32[]{:S(2)}, u32[]{:S(2)}) %all-to-all-start.3) | async-done | bytes 131104 | tf_op jit(solution)/shard_map/all_to_all | solution.py:222
  119.0 0.1 broadcast_in_dim.20
  119.1 10.0 %all_to_all.33 = f32[4,80,512]{2,1,0:T(8,128)S(1)} all-to-all(f32[4,80,512]{2,1,0:T(8,128)S(1)} %broadcast_in_dim.20), channel_id=1, replica_groups={{0,16,32,48},{64,80,96,112},{128,144,160,176},{192,208,224,240},{256,27..., dimensions={0} | all-to-all | bytes 1310720 | tf_op jit(solution)/shard_map/all_to_all | solution.py:222
  129.1 1.1 broadcast_in_dim.41
  130.2 4.1 %all-to-all-start.5 = ((f32[8,64,512]{2,1,0:T(8,128)}), f32[8,64,512]{2,1,0:T(8,128)S(1)}, u32[]{:S(2)}, u32[]{:S(2)}) async-start(f32[8,64,512]{2,1,0:T(8,128)} %broadcast_in_dim.41), calls=%async_computation.5 | async-start | bytes 2097152 | tf_op jit(solution)/shard_map/all_to_all | solution.py:222
  134.3 7.1 %collective-permute-start.8 = (f32[4,64,512]{2,1,0:T(8,128)S(1)}, f32[4,64,512]{2,1,0:T(8,128)S(1)}, u32[]{:S(2)}, u32[]{:S(2)}) collective-permute-start(f32[4,64,512]{2,1,0:T(8,128)S(1)} %slice.69.gram_ref), channel_id=1, source_target_pairs={{0,1},{1,0},{2,3},{3,2},{4,5},{5,4},{6,7},{7,6},{8,9},{9,8},{10,11... | collective-permute-start | bytes 1572872 | tf_op jit(solution)/shard_map/ppermute | solution.py:273
  141.4 1.3 collective-permute-done.8.pair_ref
  142.7 20.8 %shard_map.31.inverse_ref = f32[512,512]{1,0:T(8,128)S(1)} custom-call(s32[1]{0:T(128)S(6)} %select_n.22.core_ref, f32[4,64,512]{2,1,0:T(8,128)S(1)} %slice.69.gram_ref, f32[4,64,512]{2,1,0:T(8,128)S(1)} %collective-permute-done.8.pair_ref), custom_call_target="tpu_custom_call" | custom-call | flops 1073741824 | bytes 8388608 | tf_op jit(solution)/shard_map/pallas_call | solution.py:180
  163.6 0.0 copy-start.3
  163.6 1.0 copy-done.3
  164.6 0.0 all-to-all-done.5
  164.6 0.0 copy-start.4
  164.6 1.0 copy-done.4
  165.6 7.5 %shard_map.32 = (f32[1024,512]{1,0:T(8,128)}, f32[512,512]{1,0:T(8,128)}) custom-call(s32[1]{0:T(128)} %bitcast.column_ref, f32[1024,512]{1,0:T(8,128)} %snap_ref.3, f32[1024,256]{1,0:T(8,128)} %bitcast.8, f32[1024,256]{1,0:T(8,128)} %copy-done.2, f32[512,512]{1,0:T(8,128)} %copy-done.3, f32[8,4,16,512]{3,2,1,0:T(8,128)} %bitcast.10), custom_call_target="tpu_custom_call" | custom-call | flops 4294967296 | bytes 8388608 | tf_op jit(solution)/shard_map/pallas_call | solution.py:201
  (11 shorter events, 0.2 us)
Async XLA Ops:
  1.9 16.1 %collective-permute-start = (f32[128,256]{1,0:T(8,128)S(1)}, f32[128,256]{1,0:T(8,128)S(1)}, u32[]{:S(2)}, u32[]{:S(2)}) collective-permute-start(f32[128,256]{1,0:T(8,128)S(1)} %get-tuple-element.2), channel_id=1, source_target_pairs={{0,2},{1,3},{16,18},{17,19},{32,34},{33,35},{48,50},{49,51},{64,66... | collective-permute-start | bytes 393224 | tf_op jit(solution)/shard_map/ppermute | solution.py:246
  6.8 12.6 %collective-permute-start.6 = (f32[128,256]{1,0:T(8,128)S(1)}, f32[128,256]{1,0:T(8,128)S(1)}, u32[]{:S(2)}, u32[]{:S(2)}) collective-permute-start(f32[128,256]{1,0:T(8,128)S(1)} %get-tuple-element.3), channel_id=1, source_target_pairs={{0,14},{1,15},{16,30},{17,31},{32,46},{33,47},{48,62},{49,63},{64,... | collective-permute-start | bytes 393224 | tf_op jit(solution)/shard_map/ppermute | solution.py:246
  14.1 7.2 %collective-permute-start.5 = (f32[128,256]{1,0:T(8,128)S(1)}, f32[128,256]{1,0:T(8,128)S(1)}, u32[]{:S(2)}, u32[]{:S(2)}) collective-permute-start(f32[128,256]{1,0:T(8,128)S(1)} %get-tuple-element.4), channel_id=1, source_target_pairs={{0,12},{1,13},{16,28},{17,29},{32,44},{33,45},{48,60},{49,61},{64,... | collective-permute-start | bytes 393224 | tf_op jit(solution)/shard_map/ppermute | solution.py:246
  15.4 6.5 %collective-permute-start.4 = (f32[128,256]{1,0:T(8,128)S(1)}, f32[128,256]{1,0:T(8,128)S(1)}, u32[]{:S(2)}, u32[]{:S(2)}) collective-permute-start(f32[128,256]{1,0:T(8,128)S(1)} %get-tuple-element.5), channel_id=1, source_target_pairs={{0,10},{1,11},{16,26},{17,27},{32,42},{33,43},{48,58},{49,59},{64,... | collective-permute-start | bytes 393224 | tf_op jit(solution)/shard_map/ppermute | solution.py:246
  16.7 5.2 %collective-permute-start.3 = (f32[128,256]{1,0:T(8,128)S(1)}, f32[128,256]{1,0:T(8,128)S(1)}, u32[]{:S(2)}, u32[]{:S(2)}) collective-permute-start(f32[128,256]{1,0:T(8,128)S(1)} %get-tuple-element.6), channel_id=1, source_target_pairs={{0,8},{1,9},{16,24},{17,25},{32,40},{33,41},{48,56},{49,57},{64,72... | collective-permute-start | bytes 393224 | tf_op jit(solution)/shard_map/ppermute | solution.py:246
  18.1 4.9 %collective-permute-start.2 = (f32[128,256]{1,0:T(8,128)S(1)}, f32[128,256]{1,0:T(8,128)S(1)}, u32[]{:S(2)}, u32[]{:S(2)}) collective-permute-start(f32[128,256]{1,0:T(8,128)S(1)} %get-tuple-element.7), channel_id=1, source_target_pairs={{0,6},{1,7},{16,22},{17,23},{32,38},{33,39},{48,54},{49,55},{64,70... | collective-permute-start | bytes 393224 | tf_op jit(solution)/shard_map/ppermute | solution.py:246
  19.4 6.4 %collective-permute-start.1 = (f32[128,256]{1,0:T(8,128)S(1)}, f32[128,256]{1,0:T(8,128)}, u32[]{:S(2)}, u32[]{:S(2)}) collective-permute-start(f32[128,256]{1,0:T(8,128)S(1)} %get-tuple-element.8), channel_id=1, source_target_pairs={{0,4},{1,5},{16,20},{17,21},{32,36},{33,37},{48,52},{49,53},{64,68... | collective-permute-start | bytes 393224 | tf_op jit(solution)/shard_map/ppermute | solution.py:246
  21.3 43.8 %copy-start.1 = (f32[1024,512]{1,0:T(8,128)S(1)}, f32[1024,512]{1,0:T(8,128)}, u32[]{:S(2)}) copy-start(f32[1024,512]{1,0:T(8,128)} %snap_ref.3) | copy-start | bytes 6291460
  57.2 11.5 %copy-start = (f32[8,128,256]{2,1,0:T(8,128)}, f32[8,128,256]{2,1,0:T(8,128)S(1)}, u32[]{:S(2)}) copy-start(f32[8,128,256]{2,1,0:T(8,128)S(1)} %all_to_all.30) | copy-start | bytes 3145732
  57.2 7.9 %collective-permute-start.7 = (f32[1024,256]{1,0:T(8,128)S(1)}, f32[1024,256]{1,0:T(8,128)S(1)}, u32[]{:S(2)}, u32[]{:S(2)}) collective-permute-start(f32[1024,256]{1,0:T(8,128)S(1)} %bitcast.6), channel_id=1, source_target_pairs={{0,1},{1,0},{2,3},{3,2},{4,5},{5,4},{6,7},{7,6},{8,9},{9,8},{10,11... | collective-permute-start | bytes 3145736 | tf_op jit(solution)/shard_map/ppermute | solution.py:251
  65.1 3.6 %copy-start.2 = (f32[1024,256]{1,0:T(8,128)}, f32[1024,256]{1,0:T(8,128)S(1)}, u32[]{:S(2)}) copy-start(f32[1024,256]{1,0:T(8,128)S(1)} %collective-permute-done.7.other_ref) | copy-start | bytes 3145732
  107.7 11.3 %all-to-all-start.3 = ((f32[8,8,512]{2,1,0:T(8,128)}), f32[8,8,512]{2,1,0:T(8,128)S(1)}, u32[]{:S(2)}, u32[]{:S(2)}) async-start(f32[8,8,512]{2,1,0:T(8,128)} %broadcast_in_dim.19), calls=%async_computation.3 | async-start | bytes 262144 | tf_op jit(solution)/shard_map/all_to_all | solution.py:222
  130.2 34.3 %all-to-all-start.5 = ((f32[8,64,512]{2,1,0:T(8,128)}), f32[8,64,512]{2,1,0:T(8,128)S(1)}, u32[]{:S(2)}, u32[]{:S(2)}) async-start(f32[8,64,512]{2,1,0:T(8,128)} %broadcast_in_dim.41), calls=%async_computation.5 | async-start | bytes 2097152 | tf_op jit(solution)/shard_map/all_to_all | solution.py:222
  134.3 8.4 %collective-permute-start.8 = (f32[4,64,512]{2,1,0:T(8,128)S(1)}, f32[4,64,512]{2,1,0:T(8,128)S(1)}, u32[]{:S(2)}, u32[]{:S(2)}) collective-permute-start(f32[4,64,512]{2,1,0:T(8,128)S(1)} %slice.69.gram_ref), channel_id=1, source_target_pairs={{0,1},{1,0},{2,3},{3,2},{4,5},{5,4},{6,7},{7,6},{8,9},{9,8},{10,11... | collective-permute-start | bytes 1572872 | tf_op jit(solution)/shard_map/ppermute | solution.py:273
  163.6 1.0 copy-start.3
  164.6 1.0 copy-start.4
